TPU v7x, 32 devices: a whole 2x2x4 slice. The times are simulated.
32 devices in a mesh: parts: 2 (over y), blk: 4 (over z), grp: 4 (over x, core).
Axes of the slice: x: 2, y: 2, z: 4, core: 2. Of those that a mesh axis runs over, the one named last changes fastest.
Arguments:
- factors: float32 [64, 4096], P(None, ('parts', 'blk', 'grp')), parts along dimension 1, may hold values from -1 to 1
- tangent: float32 [64, 4096], P(None, ('parts', 'blk', 'grp')), parts along dimension 1, may hold values from -15 to 15
- counts: int32 [4096, 2048], P(('parts', 'blk', 'grp')), parts along dimension 0, may hold values from 0 to 4, as said below
Outputs:
- hess_vec: float32 [64, 4096], P(None, ('parts', 'blk', 'grp')), parts along dimension 1
- residual: float32 [64, 4096], P(None, ('parts', 'blk', 'grp')), parts along dimension 1
- inner: float32 [4], P('parts'), parts along dimension 0
There are 2 independent parts, one for each index of `parts`. A program takes and returns all parts, laid end to end along the dimension named above; each array names one. Nothing has to cross between parts.
Inputs may be any that keep to these rules, and one draw needn't show every extreme that they name: counts is symmetric.
All inputs are finite; a program needn't handle non-finite values.
Results may differ from a plain program's by a relative error of at most 0.0003.
Values sent between devices are 32-bit elements; how exact they have to be, the bound alone decides.
No kernel may reach another device: no remote copies, remote signals or barrier semaphores. Data moves between devices by JAX's collectives and lax.ppermute only.
A program may use at most 128 MiB of HBM per device.

v0:
```python
import jax
import jax.numpy as jnp
from jax import lax
from jax.sharding import PartitionSpec as P


def local(factors, tangent, counts):
    rows = counts.shape[0]
    nodes = counts.shape[1]
    scale = 1.0 / jnp.sqrt(jnp.float32(nodes))
    highest = lax.Precision.HIGHEST
    contract = (((0,), (0,)), ((), ()))
    right = (((1,), (1,)), ((), ()))
    row_start = (lax.axis_index("blk") * lax.axis_size("grp") + lax.axis_index("grp")) * rows
    row_ids = row_start + jnp.arange(rows, dtype=jnp.int32)[:, None]
    group_u, group_v = (
        lax.all_gather(factors, "grp", axis=1, tiled=True),
        lax.all_gather(tangent, "grp", axis=1, tiled=True),
    )
    piece_u = lax.all_gather(group_u, "blk", axis=1, tiled=True)
    piece_v = lax.all_gather(group_v, "blk", axis=1, tiled=True)
    width = piece_u.shape[1]
    eta = lax.dot_general(factors, piece_u, contract, precision=highest)
    deta = lax.dot_general(factors, piece_v, contract, precision=highest) + lax.dot_general(
        tangent, piece_u, contract, precision=highest
    )
    col_ids = jnp.arange(width, dtype=jnp.int32)[None, :]
    keep = row_ids != col_ids
    rate = jnp.where(keep, jnp.exp(eta), jnp.float32(0.0))
    weight = rate * deta
    tile_counts = counts.astype(jnp.float32)
    slack = jnp.where(keep, tile_counts - rate, jnp.float32(0.0))
    hess_acc = lax.dot_general(piece_u, weight, right, precision=highest)
    resid_acc = lax.dot_general(piece_u, slack - weight, right, precision=highest)
    hess_acc, resid_acc = (hess_acc, resid_acc)
    hess_vec = hess_acc * scale
    residual = resid_acc * scale
    sum_sq, sum_curv = lax.psum(
        (jnp.sum(residual * residual), jnp.sum(tangent * hess_vec)), ("blk", "grp")
    )
    inner = jnp.stack([sum_sq, sum_curv])
    return (hess_vec, residual, inner)


def solution(mesh):
    return jax.shard_map(
        local,
        mesh=mesh,
        in_specs=(
            P(None, ("parts", "blk", "grp")),
            P(None, ("parts", "blk", "grp")),
            P(("parts", "blk", "grp"), None),
        ),
        out_specs=(P(None, ("parts", "blk", "grp")), P(None, ("parts", "blk", "grp")), P("parts")),
        check_vma=False,
    )
```

profile of v0, /device:TPU:0, one launch (start us, length us, event | category | flops | bytes accessed | tf_op | source)
XLA Modules:
  0.0 85.9 jit_solution(17943244656120877728)
XLA Ops:
  0.6 0.0 copy-start.1
  0.7 6.7 %all_gather.12 = f32[64,512]{1,0:T(8,128)S(1)} all-gather(f32[64,128]{1,0:T(8,128)} %param.3), channel_id=1, replica_groups=mesh['parts'=2,'blk'=4,'grp'=4] {'grp'}, dimensions={1}, use_global_device_ids=true | all-gather | bytes 163840 | tf_op jit(solution)/shard_map/all_gather | solution.py:17
  7.4 0.0 copy-done.1
  7.4 5.6 %all_gather.14 = f32[64,512]{1,0:T(8,128)S(1)} all-gather(f32[64,128]{1,0:T(8,128)S(1)} %copy-done.1), channel_id=1, replica_groups=mesh['parts'=2,'blk'=4,'grp'=4] {'grp'}, dimensions={1}, use_global_device_ids=true | all-gather | bytes 163840 | tf_op jit(solution)/shard_map/all_gather | solution.py:18
  12.9 16.6 %all_gather.13 = f32[64,2048]{1,0:T(8,128)S(1)} all-gather(f32[64,512]{1,0:T(8,128)S(1)} %all_gather.12), channel_id=1, replica_groups=mesh['parts'=2,'blk'=4,'grp'=4] {'blk'}, dimensions={1}, use_global_device_ids=true | all-gather | bytes 655360 | tf_op jit(solution)/shard_map/all_gather | solution.py:20
  29.5 0.0 copy-start.2
  29.5 16.0 %all_gather.15 = f32[64,2048]{1,0:T(8,128)S(1)} all-gather(f32[64,512]{1,0:T(8,128)S(1)} %all_gather.14), channel_id=1, replica_groups=mesh['parts'=2,'blk'=4,'grp'=4] {'blk'}, dimensions={1}, use_global_device_ids=true | all-gather | bytes 655360 | tf_op jit(solution)/shard_map/all_gather | solution.py:21
  45.5 0.0 copy-done.2
  45.5 1.0 %fusion.11 = f32[128,2048]{1,0:T(8,128)S(1)} fusion(f32[64,128]{1,0:T(8,128)S(1)} %copy-done.2, f32[64,2048]{1,0:T(8,128)S(1)} %all_gather.15), kind=kOutput, calls=%fused_computation.20 | convolution fusion | flops 201326592 | bytes 1605632 | tf_op jit(solution)/shard_map/dot_general | solution.py:24
  46.6 1.1 %fusion.1 = f32[128,2048]{1,0:T(8,128)S(1)} fusion(f32[64,128]{1,0:T(8,128)S(1)} %copy-done.2, f32[64,2048]{1,0:T(8,128)S(1)} %all_gather.13, s32[128]{0:T(128)S(1)} %iota_add_fusion), kind=kOutput, calls=%fused_computation.3 | convolution fusion | flops 201850880 | bytes 1606144 | tf_op jit(solution)/shard_map/dot_general | solution.py:23
  47.7 0.0 copy-start
  47.7 1.1 %fusion = f32[128,2048]{1,0:T(8,128)S(1)} fusion(f32[128,2048]{1,0:T(8,128)S(1)} %fusion.1, f32[128,2048]{1,0:T(8,128)S(1)} %fusion.11, f32[64,128]{1,0:T(8,128)S(1)} %copy-done.1, f32[64,2048]{1,0:T(8,128)S(1)} %all_gather.13), kind=kOutput, calls=%fused_computation.1 | convolution fusion | flops 201850880 | bytes 3702784 | tf_op jit(solution)/shard_map/dot_general | solution.py:24
  48.8 0.2 copy-done
  48.9 2.7 %multiply_reduce_fusion.1 = (f32[]{:T(128)}, f32[64,128]{1,0:T(8,128)}) fusion(f32[64,2048]{1,0:T(8,128)S(1)} %all_gather.13, f32[128,2048]{1,0:T(8,128)S(1)} %fusion, f32[128,2048]{1,0:T(8,128)S(1)} %fusion.1, s32[128,2048]{1,0:T(8,128)S(1)} %copy-done, s32[128]{0:T(128)S(1)} %iota_add_fusion), kind=kOutput, calls=%fused_computation.16 | convolution fusion | flops 202661888 | bytes 3703300 | tf_op jit(solution)/shard_map/dot_general | solution.py:34
  51.6 2.4 %multiply_reduce_fusion = (f32[]{:T(128)}, f32[64,128]{1,0:T(8,128)}) fusion(f32[64,128]{1,0:T(8,128)S(1)} %copy-done.1, f32[128,2048]{1,0:T(8,128)S(1)} %fusion, f32[64,2048]{1,0:T(8,128)S(1)} %all_gather.13), kind=kOutput, calls=%fused_computation.15 | convolution fusion | flops 201351168 | bytes 1638404 | tf_op jit(solution)/shard_map/dot_general | solution.py:33
  54.0 30.1 %all-reduce = (f32[1]{0:T(128)}, f32[1]{0:T(128)}) all-reduce(f32[1]{0:T(128)} %bitcast.3, f32[1]{0:T(128)} %bitcast.2), channel_id=1, replica_groups=mesh['parts'=2,'blk'=4,'grp'=4] {'blk','grp'}, use_global_device_ids=true, to_apply=%region_3.4 | all-reduce | flops 2 | bytes 16 | tf_op jit(solution)/shard_map/psum | solution.py:38
  84.2 1.8 %pad_maximum_fusion = f32[2]{0:T(128)} fusion(f32[1]{0:T(128)} %get-tuple-element.3, f32[1]{0:T(128)} %get-tuple-element.4), kind=kLoop, calls=%fused_computation.17 | loop fusion | flops 2 | bytes 16 | tf_op jit(solution)/shard_map/stack | solution.py:41
  (1 shorter events, 0.0 us)
Async XLA Ops:
  0.6 6.7 %copy-start.1 = (f32[64,128]{1,0:T(8,128)S(1)}, f32[64,128]{1,0:T(8,128)}, u32[]{:S(2)}) copy-start(f32[64,128]{1,0:T(8,128)} %param.4) | copy-start | bytes 98308
  29.5 16.0 %copy-start.2 = (f32[64,128]{1,0:T(8,128)S(1)}, f32[64,128]{1,0:T(8,128)}, u32[]{:S(2)}) copy-start(f32[64,128]{1,0:T(8,128)} %param.3) | copy-start | bytes 98308
  47.7 1.2 %copy-start = (s32[128,2048]{1,0:T(8,128)S(1)}, s32[128,2048]{1,0:T(8,128)}, u32[]{:S(2)}) copy-start(s32[128,2048]{1,0:T(8,128)} %param.5) | copy-start | bytes 3145732
where the time goes:
time: 86.3 us; the launch traced here: 85.9 us
  blocking collectives  75 us (87%)
  matrix products  8.3 us (10%)
  other arithmetic  1.78 us (2%)
    psum x1, blocking collectives, local(): lax.psum((jnp.sum(residual * residual), jnp.sum(tangent * hess_vec)), ('b...  30.1 us
    all_gather x1, blocking collectives, local(): piece_u = lax.all_gather(group_u, 'blk', axis=1, tiled=True)  16.6 us
    all_gather x1, blocking collectives, local(): piece_v = lax.all_gather(group_v, 'blk', axis=1, tiled=True)  16 us
    all_gather x1, blocking collectives, local(): lax.all_gather(factors, 'grp', axis=1, tiled=True)  6.69 us
    all_gather x1, blocking collectives, local(): lax.all_gather(tangent, 'grp', axis=1, tiled=True)  5.58 us
    dot_general x1, matrix products, local(): lax.dot_general(piece_u, slack - weight, right, precision=highest)  2.69 us
    dot_general x1, matrix products, local(): hess_acc = lax.dot_general(piece_u, weight, right, precision=highest)  2.41 us
    another operation x1, other arithmetic, local(): inner = jnp.stack([sum_sq, sum_curv])  1.78 us

commit v1 on v0

v1 whole, which is shorter than its diff:
```python
import functools

import jax
import jax.numpy as jnp
from jax import lax
from jax.experimental import pallas as pl
from jax.experimental.pallas import tpu as pltpu
from jax.sharding import PartitionSpec as P

AXES = ("blk", "grp")
F32, BF16 = jnp.float32, jnp.bfloat16


def source(index, step, size):
    if size & (size - 1) == 0:
        return index ^ step
    return (index + size - step) % size


def exchange(x, blks, grps, step_blk, step_x, step_core):
    cores = 2 if grps % 2 == 0 else 1
    chips = grps // cores
    pairs = []
    for b in range(blks):
        for g in range(grps):
            sb = source(b, step_blk, blks)
            sx = source(g // cores, step_x, chips)
            sc = source(g % cores, step_core, cores)
            pairs.append(((sb * chips + sx) * cores + sc, b * grps + g))
    return lax.ppermute(x, AXES, pairs)


def split2(x):
    hi = x.astype(BF16)
    return hi, (x - hi.astype(F32)).astype(BF16)


def split3(x):
    hi = x.astype(BF16)
    rest = x - hi.astype(F32)
    mid = rest.astype(BF16)
    return hi, mid, (rest - mid.astype(F32)).astype(BF16)


def dot(a, b):
    return lax.dot_general(a, b, (((1,), (0,)), ((), ())), preferred_element_type=F32)


def dot_t(a, b):
    return lax.dot_general(a, b, (((1,), (1,)), ((), ())), preferred_element_type=F32)


def left_operands(own, rank):
    rows = own.T
    uh, um, ul = split3(rows[:, :rank])
    vh, vm = split2(rows[:, rank:])
    none = jnp.zeros_like(uh)
    first = jnp.concatenate(
        [jnp.concatenate([uh, uh, none, none], 1), jnp.concatenate([vh, vh, uh, uh], 1)], 0
    )
    second = jnp.concatenate(
        [jnp.concatenate([um, um, none, none], 1), jnp.concatenate([vm, vm, um, um], 1)], 0
    )
    third = jnp.concatenate([ul, none, none, none], 1)
    return first, second, third, uh


def tile_terms(left, cols, tile_counts, rank, diagonal):
    first, second, third, uh_rows = left
    rows = third.shape[0]
    uh, um, ul = split3(cols[:rank])
    vh, vm = split2(cols[rank:])
    right = jnp.concatenate([uh, um, vh, vm], 0)
    both = dot(first, right) + dot(second, right)
    eta = both[:rows] + (dot(third, right) + dot(uh_rows, ul))
    deta = both[rows:]
    rate = jnp.exp(eta)
    counted = tile_counts.astype(F32)
    if diagonal:
        keep = lax.broadcasted_iota(jnp.int32, rate.shape, 0) != lax.broadcasted_iota(
            jnp.int32, rate.shape, 1
        )
        rate = jnp.where(keep, rate, 0.0)
        counted = jnp.where(keep, counted, 0.0)
    weight = rate * deta
    wh, wm = split2(weight)
    sh, sm = split2(counted - rate - weight)
    out = dot_t(jnp.concatenate([uh, um], 0), jnp.concatenate([wh, sh, wm, sm], 0))
    total = out[:rank] + out[rank:]
    total = total[:, : 2 * rows] + total[:, 2 * rows :]
    return total


def columns_of(counts_ref, place, rows):
    return counts_ref[:, pl.ds(pl.multiple_of(place * rows, rows), rows)]


def own_kernel(rank, places, *refs):
    blocks, counts_ref, out_ref = refs[:-2], refs[-2], refs[-1]
    rows = counts_ref.shape[0]
    spots = places()
    left = left_operands(blocks[0][...], rank)
    total = None
    for at in range(0, len(blocks), 2):
        group = range(at, min(at + 2, len(blocks)))
        cols = jnp.concatenate([blocks[k][...] for k in group], 1)
        tile = jnp.concatenate([columns_of(counts_ref, spots[k], rows) for k in group], 1)
        part = tile_terms(left, cols, tile, rank, at == 0)
        total = part if total is None else total + part
    out_ref[...] = total


def last_kernel(rank, places, scale, own_ref, other_ref, counts_ref, sum_ref, hess_ref, resid_ref, inner_ref):
    rows = counts_ref.shape[0]
    spots = places()
    own = own_ref[...]
    left = left_operands(own, rank)
    total = sum_ref[...]
    for at in range(0, other_ref.shape[0], 2):
        group = range(at, min(at + 2, other_ref.shape[0]))
        cols = jnp.concatenate([other_ref[k] for k in group], 1)
        tile = jnp.concatenate([columns_of(counts_ref, spots[k], rows) for k in group], 1)
        total = total + tile_terms(left, cols, tile, rank, False)
    hess = total[:, :rows] * scale
    resid = total[:, rows:] * scale
    hess_ref[...] = hess
    resid_ref[...] = resid
    sum_sq = jnp.sum(resid * resid)
    sum_curv = jnp.sum(own[rank:] * hess)
    lane = lax.broadcasted_iota(jnp.int32, inner_ref.shape, 1)
    inner_ref[...] = jnp.where(lane == 0, sum_sq, jnp.where(lane == 1, sum_curv, 0.0))


def local(factors, tangent, counts):
    rank, rows = factors.shape
    nodes = counts.shape[1]
    blks, grps = lax.axis_size("blk"), lax.axis_size("grp")
    cores = 2 if grps % 2 == 0 else 1
    chips = grps // cores
    swap = functools.partial(exchange, blks=blks, grps=grps)

    own = jnp.concatenate([factors, tangent], 0)
    steps = [(b, x) for x in range(chips) for b in range(blks)]
    blocks = {(0, 0): own}
    for b in reversed(range(1, blks)):
        blocks[b, 0] = swap(own, step_blk=b, step_x=0, step_core=0)
    for x in range(1, chips):
        for b in range(blks):
            blocks[b, x] = swap(blocks[b, 0], step_blk=0, step_x=x, step_core=0)
    blocks = [blocks[step] for step in steps]

    def places(core_step):
        b, g = lax.axis_index("blk"), lax.axis_index("grp")
        x, c = g // cores, g % cores
        return [
            (source(b, sb, blks) * chips + source(x, sx, chips)) * cores
            + source(c, core_step, cores)
            for sb, sx in steps
        ]

    vmem = pl.BlockSpec(memory_space=pltpu.VMEM)
    params = pltpu.CompilerParams(vmem_limit_bytes=40 * 1024 * 1024)
    total = pl.pallas_call(
        functools.partial(own_kernel, rank, lambda: places(0)),
        out_shape=jax.ShapeDtypeStruct((rank, 2 * rows), F32),
        in_specs=[vmem] * (len(blocks) + 1),
        out_specs=vmem,
        compiler_params=params,
        name="own_core_blocks",
    )(*blocks, counts)
    others = (
        swap(jnp.stack(blocks), step_blk=0, step_x=0, step_core=1)
        if cores == 2
        else jnp.zeros((0, 2 * rank, rows), F32)
    )
    hess_vec, residual, inner = pl.pallas_call(
        functools.partial(last_kernel, rank, lambda: places(1), 1.0 / nodes**0.5),
        out_shape=(
            jax.ShapeDtypeStruct((rank, rows), F32),
            jax.ShapeDtypeStruct((rank, rows), F32),
            jax.ShapeDtypeStruct((1, 128), F32),
        ),
        in_specs=[vmem] * 4,
        out_specs=(vmem, vmem, vmem),
        compiler_params=params,
        name="other_core_blocks",
    )(own, others, counts, total)

    for x in range(1):
        terms = [
            swap(inner, step_blk=0, step_x=sx, step_core=sc)
            for sx in range(chips)
            for sc in range(cores)
            if (sx, sc) != (0, 0)
        ]
        inner = sum(terms, inner)
        terms = [swap(inner, step_blk=sb, step_x=0, step_core=0) for sb in range(1, blks)]
        inner = sum(terms, inner)
    return hess_vec, residual, inner[0, :2]


def solution(mesh):
    part = ("parts", "blk", "grp")
    return jax.shard_map(
        local,
        mesh=mesh,
        in_specs=(P(None, part), P(None, part), P(part, None)),
        out_specs=(P(None, part), P(None, part), P("parts")),
        check_vma=False,
    )
```

time: 86.3 us -> 35.7 us (0.41)
  blocking collectives: 75 us -> 0 us
  starting transfers between devices: 0 us -> 17.2 us
  waiting for transfers between devices: 0 us -> 12.7 us
  matrix products: 8.3 us -> 0 us
  Pallas kernels: 0 us -> 3.54 us
  other arithmetic: 1.78 us -> 0.01 us
  local copies, waits for them, and re-layouts: 0.17 us -> 1.43 us
    all_gather x4 -> x0, blocking collectives: 44.9 us -> none  [the longest x1 16.6 us: local(): piece_u = lax.all_gather(group_u, 'blk', axis=1, tiled=True)]
    psum x1 -> x0, blocking collectives: 30.1 us -> none  [local(): lax.psum((jnp.sum(residual * residual), jnp.sum(tangent * hess_vec)), ('b...]
    ppermute x0 -> x14, starting transfers between devices: none -> 17.2 us  [exchange(): return lax.ppermute(x, AXES, pairs)]
    ppermute x0 -> x14, waiting for transfers between devices: none -> 12.7 us  [exchange(): return lax.ppermute(x, AXES, pairs)]
    dot_general x5 -> x0, matrix products: 8.3 us -> none  [the longest x1 2.69 us: local(): lax.dot_general(piece_u, slack - weight, right, precision=highest)]
    pallas_call x0 -> x2, Pallas kernels: none -> 3.54 us  [the longest x1 2.08 us: local(): pl.pallas_call(functools.partial(last_kernel, rank, lambda: places(1), 1....]
    another operation x1 -> x0, other arithmetic: 1.78 us -> none  [local(): inner = jnp.stack([sum_sq, sum_curv])]
  transfers between devices with their start and end apart: 0 -> 14, of which waited for: 0 -> 8; matrix products, arithmetic and copies ran while one was open for 0% -> 0% of each run, Pallas kernels for 0% -> 4%
where the time goes in v1:
time: 35.7 us; the launch traced here: 35.6 us
  starting transfers between devices  17.2 us (48%)
  waiting for transfers between devices  12.7 us (36%)
  Pallas kernels  3.54 us (10%)
  local copies, waits for them, and re-layouts  1.43 us (4%)
  between operations  0.72 us (2%)
    ppermute x14, starting transfers between devices, exchange(): return lax.ppermute(x, AXES, pairs)  17.2 us
    ppermute x14, waiting for transfers between devices, exchange(): return lax.ppermute(x, AXES, pairs)  12.7 us
    pallas_call x1, Pallas kernels, local(): pl.pallas_call(functools.partial(last_kernel, rank, lambda: places(1), 1....  2.08 us
    pallas_call x1, Pallas kernels, local(): pl.pallas_call(functools.partial(own_kernel, rank, lambda: places(0)), ou...  1.46 us
    unnamed x12, local copies, waits for them, and re-layouts  0.9 us
  transfers between devices with their start and end apart: 14, of which 8 were waited for; matrix products, arithmetic and copies ran while one was open for 0% of the time, Pallas kernels for 4%

profile of v1, /device:TPU:0, one launch (start us, length us, event | category | flops | bytes accessed | tf_op | source)
XLA Modules:
  0.0 35.6 jit_solution(17034925461624035957)
XLA Ops:
  0.6 0.0 copy-start.1
  0.6 0.0 copy-start
  0.7 0.8 %constant_dynamic-update-slice_fusion.1 = f32[128,128]{1,0:T(8,128)S(1)} fusion(f32[64,128]{1,0:T(8,128)} %param.3), kind=kLoop, calls=%fused_computation.9 | loop fusion | bytes 65536
  1.5 0.0 copy-done.1
  1.5 3.1 %collective-permute-start = (f32[128,128]{1,0:T(8,128)S(1)}, f32[128,128]{1,0:T(8,128)S(1)}, u32[]{:S(2)}, u32[]{:S(2)}) collective-permute-start(f32[128,128]{1,0:T(8,128)S(1)} %constant_dynamic-update-slice_fusion.refs_0_.own_ref), channel_id=1, source_target_pairs={{4,0},{5,1},{6,2},{7,3},{0,4},{1,5},{2,6},{3,7},{12,8},{13,9},{14,... | collective-permute-start | bytes 196616 | tf_op jit(solution)/shard_map/ppermute | solution.py:30
  4.6 2.6 %collective-permute-start.1 = (f32[128,128]{1,0:T(8,128)S(1)}, f32[128,128]{1,0:T(8,128)S(1)}, u32[]{:S(2)}, u32[]{:S(2)}) collective-permute-start(f32[128,128]{1,0:T(8,128)S(1)} %constant_dynamic-update-slice_fusion.refs_0_.own_ref), channel_id=1, source_target_pairs={{8,0},{9,1},{10,2},{11,3},{12,4},{13,5},{14,6},{15,7},{0,8},{1,9},... | collective-permute-start | bytes 196616 | tf_op jit(solution)/shard_map/ppermute | solution.py:30
  7.2 0.0 collective-permute-start.2
  7.2 1.7 %collective-permute-start.3 = (f32[128,128]{1,0:T(8,128)S(1)}, f32[128,128]{1,0:T(8,128)S(1)}, u32[]{:S(2)}, u32[]{:S(2)}) collective-permute-start(f32[128,128]{1,0:T(8,128)S(1)} %constant_dynamic-update-slice_fusion.refs_0_.own_ref), channel_id=1, source_target_pairs={{2,0},{3,1},{0,2},{1,3},{6,4},{7,5},{4,6},{5,7},{10,8},{11,9},{8,1... | collective-permute-start | bytes 196616 | tf_op jit(solution)/shard_map/ppermute | solution.py:30
  8.9 0.0 collective-permute-done.refs_1_
  8.9 0.4 %collective-permute-start.4 = (f32[128,128]{1,0:T(8,128)S(1)}, f32[128,128]{1,0:T(8,128)S(1)}, u32[]{:S(2)}, u32[]{:S(2)}) collective-permute-start(f32[128,128]{1,0:T(8,128)S(1)} %collective-permute-done.refs_1_), channel_id=1, source_target_pairs={{2,0},{3,1},{0,2},{1,3},{6,4},{7,5},{4,6},{5,7},{10,8},{11,9},{8,1... | collective-permute-start | bytes 196616 | tf_op jit(solution)/shard_map/ppermute | solution.py:30
  9.3 2.6 %collective-permute-done.1.refs_2_ = f32[128,128]{1,0:T(8,128)S(1)} collective-permute-done((f32[128,128]{1,0:T(8,128)S(1)}, f32[128,128]{1,0:T(8,128)S(1)}, u32[]{:S(2)}, u32[]{:S(2)}) %collective-permute-start.1) | collective-permute-done | bytes 65568 | tf_op jit(solution)/shard_map/ppermute | solution.py:30
  11.9 1.5 %collective-permute-start.5 = (f32[128,128]{1,0:T(8,128)S(1)}, f32[128,128]{1,0:T(8,128)S(1)}, u32[]{:S(2)}, u32[]{:S(2)}) collective-permute-start(f32[128,128]{1,0:T(8,128)S(1)} %collective-permute-done.1.refs_2_), channel_id=1, source_target_pairs={{2,0},{3,1},{0,2},{1,3},{6,4},{7,5},{4,6},{5,7},{10,8},{11,9},{8,1... | collective-permute-start | bytes 196616 | tf_op jit(solution)/shard_map/ppermute | solution.py:30
  13.4 0.0 collective-permute-done.2.refs_3_
  13.4 1.4 %collective-permute-start.6 = (f32[128,128]{1,0:T(8,128)S(1)}, f32[128,128]{1,0:T(8,128)S(1)}, u32[]{:S(2)}, u32[]{:S(2)}) collective-permute-start(f32[128,128]{1,0:T(8,128)S(1)} %collective-permute-done.2.refs_3_), channel_id=1, source_target_pairs={{2,0},{3,1},{0,2},{1,3},{6,4},{7,5},{4,6},{5,7},{10,8},{11,9},{8,1... | collective-permute-start | bytes 196616 | tf_op jit(solution)/shard_map/ppermute | solution.py:30
  14.8 0.0 collective-permute-done.3.refs_4_
  14.8 0.0 collective-permute-done.4.refs_5_
  14.8 1.3 %collective-permute-done.5.refs_6_ = f32[128,128]{1,0:T(8,128)S(1)} collective-permute-done((f32[128,128]{1,0:T(8,128)S(1)}, f32[128,128]{1,0:T(8,128)S(1)}, u32[]{:S(2)}, u32[]{:S(2)}) %collective-permute-start.5) | collective-permute-done | bytes 65568 | tf_op jit(solution)/shard_map/ppermute | solution.py:30
  16.1 1.6 %collective-permute-done.6.refs_7_ = f32[128,128]{1,0:T(8,128)S(1)} collective-permute-done((f32[128,128]{1,0:T(8,128)S(1)}, f32[128,128]{1,0:T(8,128)S(1)}, u32[]{:S(2)}, u32[]{:S(2)}) %collective-permute-start.6) | collective-permute-done | bytes 65568 | tf_op jit(solution)/shard_map/ppermute | solution.py:30
  17.7 0.0 collective-permute-start.7
  17.7 0.0 copy-done
  17.7 1.5 %own_core_blocks.1.sum_ref = f32[64,256]{1,0:T(8,128)S(1)} custom-call(f32[128,128]{1,0:T(8,128)S(1)} %constant_dynamic-update-slice_fusion.refs_0_.own_ref, f32[128,128]{1,0:T(8,128)S(1)} %collective-permute-done.refs_1_, f32[128,128]{1,0:T(8,128)S(1)} %collective-permute-done.1.refs_2_, f32[128,128]{1,0:T(8,128)S(1)} %collective-permute-done.2.refs_3_, ...), custom_call_target="tpu_custom_call" | custom-call | tf_op jit(solution)/shard_map/own_core_blocks/pallas_call | solution.py:163
  19.2 0.4 %collective-permute-done.7.other_ref = f32[8,128,128]{2,1,0:T(8,128)S(1)} collective-permute-done((f32[8,128,128]{2,1,0:T(8,128)S(1)}, f32[8,128,128]{2,1,0:T(8,128)S(1)}, u32[]{:S(2)}, u32[]{:S(2)}) %collective-permute-start.7) | collective-permute-done | bytes 524320 | tf_op jit(solution)/shard_map/ppermute | solution.py:30
  19.6 2.1 %other_core_blocks.1 = (f32[64,128]{1,0:T(8,128)}, f32[64,128]{1,0:T(8,128)}, f32[1,128]{1,0:T(1,128)S(1)}) custom-call(f32[128,128]{1,0:T(8,128)S(1)} %constant_dynamic-update-slice_fusion.refs_0_.own_ref, f32[8,128,128]{2,1,0:T(8,128)S(1)} %collective-permute-done.7.other_ref, s32[128,2048]{1,0:T(8,128)S(1)} %copy-done, f32[64,256]{1,0:T(8,128)S(1)} %own_core_blocks.1.sum_ref), custom_call_target="tpu_custom_call" | custom-call | tf_op jit(solution)/shard_map/other_core_blocks/pallas_call | solution.py:176
  21.7 1.1 %collective-permute-start.10 = (f32[1,128]{1,0:T(1,128)S(1)}, f32[1,128]{1,0:T(1,128)S(1)}, u32[]{:S(2)}, u32[]{:S(2)}) collective-permute-start(f32[1,128]{1,0:T(1,128)S(1)} %get-tuple-element.8), channel_id=1, source_target_pairs={{3,0},{2,1},{1,2},{0,3},{7,4},{6,5},{5,6},{4,7},{11,8},{10,9},{9,1... | collective-permute-start | bytes 1544 | tf_op jit(solution)/shard_map/ppermute | solution.py:30
  22.8 0.4 %collective-permute-start.8 = (f32[1,128]{1,0:T(1,128)S(1)}, f32[1,128]{1,0:T(1,128)S(1)}, u32[]{:S(2)}, u32[]{:S(2)}) collective-permute-start(f32[1,128]{1,0:T(1,128)S(1)} %get-tuple-element.8), channel_id=1, source_target_pairs={{1,0},{0,1},{3,2},{2,3},{5,4},{4,5},{7,6},{6,7},{9,8},{8,9},{11,10... | collective-permute-start | bytes 1544 | tf_op jit(solution)/shard_map/ppermute | solution.py:30
  23.1 0.7 %collective-permute-start.9 = (f32[1,128]{1,0:T(1,128)S(1)}, f32[1,128]{1,0:T(1,128)S(1)}, u32[]{:S(2)}, u32[]{:S(2)}) collective-permute-start(f32[1,128]{1,0:T(1,128)S(1)} %get-tuple-element.8), channel_id=1, source_target_pairs={{2,0},{3,1},{0,2},{1,3},{6,4},{7,5},{4,6},{5,7},{10,8},{11,9},{8,1... | collective-permute-start | bytes 1544 | tf_op jit(solution)/shard_map/ppermute | solution.py:30
  23.8 0.8 %collective-permute-done.10 = f32[1,128]{1,0:T(1,128)S(1)} collective-permute-done((f32[1,128]{1,0:T(1,128)S(1)}, f32[1,128]{1,0:T(1,128)S(1)}, u32[]{:S(2)}, u32[]{:S(2)}) %collective-permute-start.10) | collective-permute-done | bytes 544 | tf_op jit(solution)/shard_map/ppermute | solution.py:30
  24.7 0.0 collective-permute-done.8
  24.7 2.0 %collective-permute-done.9 = f32[1,128]{1,0:T(1,128)S(1)} collective-permute-done((f32[1,128]{1,0:T(1,128)S(1)}, f32[1,128]{1,0:T(1,128)S(1)}, u32[]{:S(2)}, u32[]{:S(2)}) %collective-permute-start.9) | collective-permute-done | bytes 544 | tf_op jit(solution)/shard_map/ppermute | solution.py:30
  26.7 0.0 collective-permute-start.11
  26.7 3.0 %collective-permute-start.12 = (f32[1,128]{1,0:T(1,128)S(1)}, f32[1,128]{1,0:T(1,128)S(1)}, u32[]{:S(2)}, u32[]{:S(2)}) collective-permute-start(f32[1,128]{1,0:T(1,128)S(1)} %add_add_fusion.1), channel_id=1, source_target_pairs={{8,0},{9,1},{10,2},{11,3},{12,4},{13,5},{14,6},{15,7},{0,8},{1,9},... | collective-permute-start | bytes 1544 | tf_op jit(solution)/shard_map/ppermute | solution.py:30
  29.7 1.3 %collective-permute-start.13 = (f32[1,128]{1,0:T(1,128)S(1)}, f32[1,128]{1,0:T(1,128)S(1)}, u32[]{:S(2)}, u32[]{:S(2)}) collective-permute-start(f32[1,128]{1,0:T(1,128)S(1)} %add_add_fusion.1), channel_id=1, source_target_pairs={{12,0},{13,1},{14,2},{15,3},{8,4},{9,5},{10,6},{11,7},{4,8},{5,9},... | collective-permute-start | bytes 1544 | tf_op jit(solution)/shard_map/ppermute | solution.py:30
  31.1 0.0 collective-permute-done.11
  31.1 0.2 collective-permute-done.12
  31.2 3.8 %collective-permute-done.13 = f32[1,128]{1,0:T(1,128)S(1)} collective-permute-done((f32[1,128]{1,0:T(1,128)S(1)}, f32[1,128]{1,0:T(1,128)S(1)}, u32[]{:S(2)}, u32[]{:S(2)}) %collective-permute-start.13) | collective-permute-done | bytes 544 | tf_op jit(solution)/shard_map/ppermute | solution.py:30
  35.1 0.5 %slice_bitcast_fusion = f32[2]{0:T(128)} fusion(f32[1,128]{1,0:T(1,128)S(1)} %add_add_fusion), kind=kLoop, calls=%fused_computation.10 | loop fusion | bytes 16 | tf_op jit(solution)/shard_map/squeeze | solution.py:199
  (11 shorter events, 0.1 us)
Async XLA Ops:
  0.6 0.9 %copy-start.1 = (f32[64,128]{1,0:T(8,128)S(1)}, f32[64,128]{1,0:T(8,128)}, u32[]{:S(2)}) copy-start(f32[64,128]{1,0:T(8,128)} %param.4) | copy-start | bytes 98308
  0.6 17.1 %copy-start = (s32[128,2048]{1,0:T(8,128)S(1)}, s32[128,2048]{1,0:T(8,128)}, u32[]{:S(2)}) copy-start(s32[128,2048]{1,0:T(8,128)} %counts_ref.1) | copy-start | bytes 3145732
  1.5 7.4 %collective-permute-start = (f32[128,128]{1,0:T(8,128)S(1)}, f32[128,128]{1,0:T(8,128)S(1)}, u32[]{:S(2)}, u32[]{:S(2)}) collective-permute-start(f32[128,128]{1,0:T(8,128)S(1)} %constant_dynamic-update-slice_fusion.refs_0_.own_ref), channel_id=1, source_target_pairs={{4,0},{5,1},{6,2},{7,3},{0,4},{1,5},{2,6},{3,7},{12,8},{13,9},{14,... | collective-permute-start | bytes 196616 | tf_op jit(solution)/shard_map/ppermute | solution.py:30
  4.6 7.3 %collective-permute-start.1 = (f32[128,128]{1,0:T(8,128)S(1)}, f32[128,128]{1,0:T(8,128)S(1)}, u32[]{:S(2)}, u32[]{:S(2)}) collective-permute-start(f32[128,128]{1,0:T(8,128)S(1)} %constant_dynamic-update-slice_fusion.refs_0_.own_ref), channel_id=1, source_target_pairs={{8,0},{9,1},{10,2},{11,3},{12,4},{13,5},{14,6},{15,7},{0,8},{1,9},... | collective-permute-start | bytes 196616 | tf_op jit(solution)/shard_map/ppermute | solution.py:30
  7.2 6.2 %collective-permute-start.2 = (f32[128,128]{1,0:T(8,128)S(1)}, f32[128,128]{1,0:T(8,128)S(1)}, u32[]{:S(2)}, u32[]{:S(2)}) collective-permute-start(f32[128,128]{1,0:T(8,128)S(1)} %constant_dynamic-update-slice_fusion.refs_0_.own_ref), channel_id=1, source_target_pairs={{12,0},{13,1},{14,2},{15,3},{8,4},{9,5},{10,6},{11,7},{4,8},{5,9},... | collective-permute-start | bytes 196616 | tf_op jit(solution)/shard_map/ppermute | solution.py:30
  7.2 7.6 %collective-permute-start.3 = (f32[128,128]{1,0:T(8,128)S(1)}, f32[128,128]{1,0:T(8,128)S(1)}, u32[]{:S(2)}, u32[]{:S(2)}) collective-permute-start(f32[128,128]{1,0:T(8,128)S(1)} %constant_dynamic-update-slice_fusion.refs_0_.own_ref), channel_id=1, source_target_pairs={{2,0},{3,1},{0,2},{1,3},{6,4},{7,5},{4,6},{5,7},{10,8},{11,9},{8,1... | collective-permute-start | bytes 196616 | tf_op jit(solution)/shard_map/ppermute | solution.py:30
  8.9 5.9 %collective-permute-start.4 = (f32[128,128]{1,0:T(8,128)S(1)}, f32[128,128]{1,0:T(8,128)S(1)}, u32[]{:S(2)}, u32[]{:S(2)}) collective-permute-start(f32[128,128]{1,0:T(8,128)S(1)} %collective-permute-done.refs_1_), channel_id=1, source_target_pairs={{2,0},{3,1},{0,2},{1,3},{6,4},{7,5},{4,6},{5,7},{10,8},{11,9},{8,1... | collective-permute-start | bytes 196616 | tf_op jit(solution)/shard_map/ppermute | solution.py:30
  11.9 4.3 %collective-permute-start.5 = (f32[128,128]{1,0:T(8,128)S(1)}, f32[128,128]{1,0:T(8,128)S(1)}, u32[]{:S(2)}, u32[]{:S(2)}) collective-permute-start(f32[128,128]{1,0:T(8,128)S(1)} %collective-permute-done.1.refs_2_), channel_id=1, source_target_pairs={{2,0},{3,1},{0,2},{1,3},{6,4},{7,5},{4,6},{5,7},{10,8},{11,9},{8,1... | collective-permute-start | bytes 196616 | tf_op jit(solution)/shard_map/ppermute | solution.py:30
  13.4 4.3 %collective-permute-start.6 = (f32[128,128]{1,0:T(8,128)S(1)}, f32[128,128]{1,0:T(8,128)S(1)}, u32[]{:S(2)}, u32[]{:S(2)}) collective-permute-start(f32[128,128]{1,0:T(8,128)S(1)} %collective-permute-done.2.refs_3_), channel_id=1, source_target_pairs={{2,0},{3,1},{0,2},{1,3},{6,4},{7,5},{4,6},{5,7},{10,8},{11,9},{8,1... | collective-permute-start | bytes 196616 | tf_op jit(solution)/shard_map/ppermute | solution.py:30
  17.7 1.9 %collective-permute-start.7 = (f32[8,128,128]{2,1,0:T(8,128)S(1)}, f32[8,128,128]{2,1,0:T(8,128)S(1)}, u32[]{:S(2)}, u32[]{:S(2)}) collective-permute-start(f32[8,128,128]{2,1,0:T(8,128)S(1)} %bitcast_dynamic-update-slice_fusion), channel_id=1, source_target_pairs={{1,0},{0,1},{3,2},{2,3},{5,4},{4,5},{7,6},{6,7},{9,8},{8,9},{11,10... | collective-permute-start | bytes 1572872 | tf_op jit(solution)/shard_map/ppermute | solution.py:30
  21.7 3.0 %collective-permute-start.10 = (f32[1,128]{1,0:T(1,128)S(1)}, f32[1,128]{1,0:T(1,128)S(1)}, u32[]{:S(2)}, u32[]{:S(2)}) collective-permute-start(f32[1,128]{1,0:T(1,128)S(1)} %get-tuple-element.8), channel_id=1, source_target_pairs={{3,0},{2,1},{1,2},{0,3},{7,4},{6,5},{5,6},{4,7},{11,8},{10,9},{9,1... | collective-permute-start | bytes 1544 | tf_op jit(solution)/shard_map/ppermute | solution.py:30
  22.8 1.9 %collective-permute-start.8 = (f32[1,128]{1,0:T(1,128)S(1)}, f32[1,128]{1,0:T(1,128)S(1)}, u32[]{:S(2)}, u32[]{:S(2)}) collective-permute-start(f32[1,128]{1,0:T(1,128)S(1)} %get-tuple-element.8), channel_id=1, source_target_pairs={{1,0},{0,1},{3,2},{2,3},{5,4},{4,5},{7,6},{6,7},{9,8},{8,9},{11,10... | collective-permute-start | bytes 1544 | tf_op jit(solution)/shard_map/ppermute | solution.py:30
  23.1 3.5 %collective-permute-start.9 = (f32[1,128]{1,0:T(1,128)S(1)}, f32[1,128]{1,0:T(1,128)S(1)}, u32[]{:S(2)}, u32[]{:S(2)}) collective-permute-start(f32[1,128]{1,0:T(1,128)S(1)} %get-tuple-element.8), channel_id=1, source_target_pairs={{2,0},{3,1},{0,2},{1,3},{6,4},{7,5},{4,6},{5,7},{10,8},{11,9},{8,1... | collective-permute-start | bytes 1544 | tf_op jit(solution)/shard_map/ppermute | solution.py:30
  26.7 4.4 %collective-permute-start.11 = (f32[1,128]{1,0:T(1,128)S(1)}, f32[1,128]{1,0:T(1,128)S(1)}, u32[]{:S(2)}, u32[]{:S(2)}) collective-permute-start(f32[1,128]{1,0:T(1,128)S(1)} %add_add_fusion.1), channel_id=1, source_target_pairs={{4,0},{5,1},{6,2},{7,3},{0,4},{1,5},{2,6},{3,7},{12,8},{13,9},{14,... | collective-permute-start | bytes 1544 | tf_op jit(solution)/shard_map/ppermute | solution.py:30
  26.7 4.6 %collective-permute-start.12 = (f32[1,128]{1,0:T(1,128)S(1)}, f32[1,128]{1,0:T(1,128)S(1)}, u32[]{:S(2)}, u32[]{:S(2)}) collective-permute-start(f32[1,128]{1,0:T(1,128)S(1)} %add_add_fusion.1), channel_id=1, source_target_pairs={{8,0},{9,1},{10,2},{11,3},{12,4},{13,5},{14,6},{15,7},{0,8},{1,9},... | collective-permute-start | bytes 1544 | tf_op jit(solution)/shard_map/ppermute | solution.py:30
  29.7 5.3 %collective-permute-start.13 = (f32[1,128]{1,0:T(1,128)S(1)}, f32[1,128]{1,0:T(1,128)S(1)}, u32[]{:S(2)}, u32[]{:S(2)}) collective-permute-start(f32[1,128]{1,0:T(1,128)S(1)} %add_add_fusion.1), channel_id=1, source_target_pairs={{12,0},{13,1},{14,2},{15,3},{8,4},{9,5},{10,6},{11,7},{4,8},{5,9},... | collective-permute-start | bytes 1544 | tf_op jit(solution)/shard_map/ppermute | solution.py:30

commit v2 on v0

v2 whole, which is shorter than its diff:
```python
import functools

import jax
import jax.numpy as jnp
from jax import lax
from jax.experimental import pallas as pl
from jax.experimental.pallas import tpu as pltpu
from jax.sharding import PartitionSpec as P

AXES = ("blk", "grp")
CORES = 2
FAR, NEAR = 1, 0
F32, BF16 = jnp.float32, jnp.bfloat16


def permute(x, blks, chips, moves):
    pairs = []
    for b in range(blks):
        for x_at in range(chips):
            for c in range(CORES):
                step = moves[c]
                to = ((b ^ step[0]) * chips + (x_at ^ step[1])) * CORES + (c ^ step[2])
                pairs.append(((b * chips + x_at) * CORES + c, to))
    return lax.ppermute(x, AXES, pairs)


def split2(x):
    hi = x.astype(BF16)
    return hi, (x - hi.astype(F32)).astype(BF16)


def split3(x):
    hi = x.astype(BF16)
    rest = x - hi.astype(F32)
    mid = rest.astype(BF16)
    return hi, mid, (rest - mid.astype(F32)).astype(BF16)


def dot(a, b):
    return lax.dot_general(a, b, (((1,), (0,)), ((), ())), preferred_element_type=F32)


def dot_t(a, b):
    return lax.dot_general(a, b, (((1,), (1,)), ((), ())), preferred_element_type=F32)


def schedule(blks, chips):
    half = blks // 2
    if (blks, chips) == (4, 2):
        ops = [
            (None, (3, 0, 0), (0, 1, 0)),
            (None, (2, 0, 0), (1, 0, 0)),
            (0, (0, 1, 0), (1, 0, 0)),
            (1, (0, 1, 1), (0, 0, 1)),
        ]
        return ops, [(0, 0), (1, 1), (2, 2), (None, 3)], [[0, 1], [2], [3]]
    ops, slots = [], []
    far = [(b, x) for x in range(chips) for b in range(half, blks)]
    near = [(b, x) for x in range(chips) for b in range(half)][1:] + far[-1:]
    for k in range(len(far)):
        src = k % half if k >= half else None
        (fb, fx), (nb, nx) = (far[src], near[src]) if k >= half else ((0, 0), (0, 0))
        far_move = (far[k][0] ^ fb, far[k][1] ^ fx, 0)
        near_move = (near[k][0] ^ nb, near[k][1] ^ nx, 0)
        if k == len(far) - 1:
            far_move, near_move = (*far_move[:2], 1), (0, 0, 1)
        ops.append((src, far_move, near_move))
        slots.append((k, k))
    slots[-1] = (None, len(far) - 1)
    return ops, slots, [range(half), range(half, len(far) - 1), [len(far) - 1]]


def left_kernel(rank, chip_ref, counts_ref, other_counts_ref, first_ref, second_ref, third_ref):
    span = 2 * rank
    nodes = jnp.concatenate([chip_ref[:span].T, chip_ref[span:].T], 0)
    uh, um, ul = split3(nodes[:, :rank])
    vh, vm = split2(nodes[:, rank:])
    none = jnp.zeros_like(uh)
    first_ref[...] = jnp.concatenate(
        [jnp.concatenate([uh, uh, none, none], 1), jnp.concatenate([vh, vh, uh, uh], 1)], 0
    )
    second_ref[...] = jnp.concatenate(
        [jnp.concatenate([um, um, none, none], 1), jnp.concatenate([vm, vm, um, um], 1)], 0
    )
    third_ref[...] = jnp.concatenate([ul, uh], 1)


def chip_terms(left, chip, tile_counts, rank, diagonal):
    first, second, third = left
    rows = third.shape[0]
    span = 2 * rank
    cols = jnp.concatenate([chip[:span], chip[span:]], 1)
    uh, um, ul = split3(cols[:rank])
    vh, vm = split2(cols[rank:])
    right = jnp.concatenate([uh, um, vh, vm], 0)
    eta = dot(
        jnp.concatenate([first[:rows], second[:rows], third], 1),
        jnp.concatenate([right, right, uh, ul], 0),
    )
    deta = dot(
        jnp.concatenate([first[rows:], second[rows:]], 1), jnp.concatenate([right, right], 0)
    )
    rate = jnp.exp(eta)
    counted = tile_counts.astype(F32)
    if diagonal is not None:
        at_row = lax.broadcasted_iota(jnp.int32, rate.shape, 0)
        at_col = lax.broadcasted_iota(jnp.int32, rate.shape, 1)
        keep = jnp.logical_or(at_row != at_col, jnp.logical_not(diagonal))
        rate = jnp.where(keep, rate, 0.0)
        counted = jnp.where(keep, counted, 0.0)
    weight = rate * deta
    wh, wm = split2(weight)
    sh, sm = split2(counted - rate - weight)
    out = dot_t(jnp.concatenate([uh, um], 0), jnp.concatenate([wh, sh, wm, sm], 0))
    total = out[:rank] + out[rank:]
    return total[:, : 2 * rows] + total[:, 2 * rows :]


def tile_of(counts_ref, other_counts_ref, place):
    rows = counts_ref.shape[0]
    chip, me = place
    lines = []
    for ref in (counts_ref, other_counts_ref):
        halves = [
            ref[:, pl.ds(pl.multiple_of((chip * CORES + half) * rows, rows), rows)]
            for half in (me, 1 - me)
        ]
        lines.append(jnp.concatenate(halves, 1))
    return jnp.concatenate(lines, 0)


def chips_kernel(rank, places, is_far, plan, part, *refs):
    left = [ref[...] for ref in refs[:3]]
    counts_ref, other_ref = refs[3:5]
    count = 1 + max(max(entry[:2]) for entry in plan)
    blocks = refs[5 : 5 + count]
    rest = refs[5 + count :]
    rows = counts_ref.shape[0]
    outs = 2 if part else 1
    total = rest[0][...] if len(rest) > outs else None
    far = is_far()
    for (at_far, at_near, is_own), place in zip(plan, places()):
        chip = blocks[at_far][...]
        if at_far != at_near:
            chip = jnp.where(far, chip, blocks[at_near][...])
        tile = tile_of(counts_ref, other_ref, place)
        own_core = {FAR: far, NEAR: jnp.logical_not(far), None: None}[is_own]
        terms = chip_terms(left, chip, tile, rank, own_core)
        total = terms if total is None else total + terms
    if part:
        mine_ref, theirs_ref = rest[-2:]
        mine_ref[...] = jnp.concatenate([total[:, :rows], total[:, 2 * rows : 3 * rows]], 1)
        theirs_ref[...] = jnp.concatenate([total[:, rows : 2 * rows], total[:, 3 * rows :]], 1)
    else:
        rest[-1][...] = total


def finish_kernel(rank, scale, tangent_ref, mine_ref, got_ref, hess_ref, resid_ref, inner_ref):
    rows = tangent_ref.shape[1]
    total = (mine_ref[...] + got_ref[...]) * scale
    hess, resid = total[:, :rows], total[:, rows:]
    hess_ref[...] = hess
    resid_ref[...] = resid
    sum_sq = jnp.sum(resid * resid)
    sum_curv = jnp.sum(tangent_ref[rank:] * hess)
    lane = lax.broadcasted_iota(jnp.int32, inner_ref.shape, 1)
    inner_ref[...] = jnp.where(lane == 0, sum_sq, jnp.where(lane == 1, sum_curv, 0.0))


def local(factors, tangent, counts):
    rank, rows = factors.shape
    nodes = counts.shape[1]
    blks, grps = lax.axis_size("blk"), lax.axis_size("grp")
    chips = grps // CORES
    def is_far():
        return lax.axis_index("grp") % CORES == FAR

    vmem = pl.BlockSpec(memory_space=pltpu.VMEM)
    params = pltpu.CompilerParams(vmem_limit_bytes=40 * 1024 * 1024)

    def call(kernel, name, out_shape, *args):
        return pl.pallas_call(
            kernel,
            out_shape=out_shape,
            in_specs=[vmem] * len(args),
            out_specs=jax.tree.map(lambda _: vmem, out_shape),
            compiler_params=params,
            name=name,
        )(*args)

    def shape(*dims, dtype=F32):
        return jax.ShapeDtypeStruct(dims, dtype)

    swap_cores = functools.partial(permute, blks=blks, chips=chips, moves=[(0, 0, 1)] * 2)
    own = lax.optimization_barrier(jnp.concatenate([factors, tangent], 0))
    chip = jnp.concatenate([own, swap_cores(factors), swap_cores(tangent)], 0)
    (chip, counts) = lax.optimization_barrier((chip, counts))
    other_counts = swap_cores(counts)

    ops, slots, groups = schedule(blks, chips)
    left = call(
        functools.partial(left_kernel, rank),
        "row_operands",
        tuple(
            shape(n * rows, k * rank, dtype=BF16) for n, k in ((4, 4), (4, 4), (2, 2))
        ),
        chip,
        counts,
        other_counts,
    )
    got, holds = {None: chip}, {None: {FAR: (0, 0, FAR), NEAR: (0, 0, NEAR)}}
    for k, (src, far_move, near_move) in enumerate(ops):
        if k == 2:
            (left, got[src]) = lax.optimization_barrier((left, got[src]))
        sent = {FAR: far_move, NEAR: near_move}
        got[k] = permute(got[src], blks, chips, [sent[core] for core in range(CORES)])
        holds[k] = {}
        for core in (FAR, NEAR):
            sender = core ^ sent[core][2]
            b, x, first = holds[src][sender]
            holds[k][core] = (b ^ sent[sender][0], x ^ sent[sender][1], first)

    def places(entries):
        b, g = lax.axis_index("blk"), lax.axis_index("grp")
        far, x = is_far(), g // CORES
        found = []
        for at_far, at_near in entries:
            ours, theirs = holds[at_far][FAR], holds[at_near][NEAR]
            step_b, step_x, first = (jnp.where(far, p, q) for p, q in zip(ours, theirs))
            found.append(((b ^ step_b) * chips + (x ^ step_x), first))
        return found

    total = ()
    for group in groups:
        entries = [slots[k] for k in group]
        used = []
        for entry in entries:
            used += [k for k in dict.fromkeys(entry) if k not in used]
        plan = [
            (used.index(p), used.index(q), FAR if p is None else NEAR if q is None else None)
            for p, q in entries
        ]
        part = group is groups[-1]
        total = call(
            functools.partial(
                chips_kernel, rank, functools.partial(places, entries), is_far, plan, part
            ),
            "chips_" + "_".join(map(str, group)),
            (shape(rank, 2 * rows),) * 2 if part else (shape(rank, 4 * rows),),
            *left,
            counts,
            other_counts,
            *[got[k] for k in used],
            *total,
        )
    mine, theirs = total
    hess_vec, residual, inner = call(
        functools.partial(finish_kernel, rank, 1.0 / nodes**0.5),
        "finish",
        (shape(rank, rows), shape(rank, rows), shape(1, 128)),
        own,
        mine,
        swap_cores(theirs),
    )
    size = blks * grps
    spread = jnp.broadcast_to(inner[None], (size, 1, 128))
    order = [list(range(size))[::-1]]
    inner = lax.all_to_all(spread, AXES, 0, 0, axis_index_groups=order, tiled=True).sum(0)
    return hess_vec, residual, inner[0, :2]


def solution(mesh):
    part = ("parts", "blk", "grp")
    return jax.shard_map(
        local,
        mesh=mesh,
        in_specs=(P(None, part), P(None, part), P(part, None)),
        out_specs=(P(None, part), P(None, part), P("parts")),
        check_vma=False,
    )
```

time: 86.3 us -> 29.1 us (0.34)
  blocking collectives: 75 us -> 8.45 us
  starting transfers between devices: 0 us -> 9.13 us
  matrix products: 8.3 us -> 0 us
  waiting for transfers between devices: 0 us -> 4.8 us
  Pallas kernels: 0 us -> 3.15 us
  local copies, waits for them, and re-layouts: 0.17 us -> 1.75 us
  other arithmetic: 1.78 us -> 0.81 us
    all_gather x4 -> x0, blocking collectives: 44.9 us -> none  [the longest x1 16.6 us: local(): piece_u = lax.all_gather(group_u, 'blk', axis=1, tiled=True)]
    psum x1 -> x0, blocking collectives: 30.1 us -> none  [local(): lax.psum((jnp.sum(residual * residual), jnp.sum(tangent * hess_vec)), ('b...]
    ppermute x0 -> x8, starting transfers between devices: none -> 9.13 us  [permute(): return lax.ppermute(x, AXES, pairs)]
    all_to_all x0 -> x1, blocking collectives: none -> 8.45 us  [local(): lax.all_to_all(spread, AXES, 0, 0, axis_index_groups=order, tiled=True)]
    dot_general x5 -> x0, matrix products: 8.3 us -> none  [the longest x1 2.69 us: local(): lax.dot_general(piece_u, slack - weight, right, precision=highest)]
    ppermute x0 -> x8, waiting for transfers between devices: none -> 4.8 us  [permute(): return lax.ppermute(x, AXES, pairs)]
    pallas_call x0 -> x5, Pallas kernels: none -> 3.15 us  [call(): pl.pallas_call(kernel, out_shape=out_shape, in_specs=[vmem] * len(args),...]
    another operation x1 -> x0, other arithmetic: 1.78 us -> none  [local(): inner = jnp.stack([sum_sq, sum_curv])]
  transfers between devices with their start and end apart: 0 -> 8, of which waited for: 0 -> 6; matrix products, arithmetic and copies ran while one was open for 0% -> 3% of each run, Pallas kernels for 0% -> 7%
where the time goes in v2:
time: 29.1 us; the launch traced here: 28.8 us
  starting transfers between devices  9.13 us (31%)
  blocking collectives  8.45 us (29%)
  waiting for transfers between devices  4.8 us (16%)
  Pallas kernels  3.15 us (11%)
  local copies, waits for them, and re-layouts  1.75 us (6%)
  other arithmetic  0.81 us (3%)
  between operations  0.69 us (2%)
    ppermute x8, starting transfers between devices, permute(): return lax.ppermute(x, AXES, pairs)  9.13 us
    all_to_all x1, blocking collectives, local(): lax.all_to_all(spread, AXES, 0, 0, axis_index_groups=order, tiled=True)  8.45 us
    ppermute x8, waiting for transfers between devices, permute(): return lax.ppermute(x, AXES, pairs)  4.8 us
    pallas_call x5, Pallas kernels, call(): pl.pallas_call(kernel, out_shape=out_shape, in_specs=[vmem] * len(args),...  3.15 us
    unnamed x4, local copies, waits for them, and re-layouts  1.23 us
    concatenate x1, other arithmetic, local(): own = lax.optimization_barrier(jnp.concatenate([factors, tangent], 0))  0.78 us
  transfers between devices with their start and end apart: 8, of which 6 were waited for; matrix products, arithmetic and copies ran while one was open for 3% of the time, Pallas kernels for 7%

profile of v2, /device:TPU:0, one launch (start us, length us, event | category | flops | bytes accessed | tf_op | source)
XLA Modules:
  0.0 28.8 jit_solution(2831450208582612931)
XLA Ops:
  0.6 0.5 %collective-permute-start = (f32[64,128]{1,0:T(8,128)}, f32[64,128]{1,0:T(8,128)S(1)}, u32[]{:S(2)}, u32[]{:S(2)}) collective-permute-start(f32[64,128]{1,0:T(8,128)} %param.3), channel_id=1, source_target_pairs={{0,1},{1,0},{2,3},{3,2},{4,5},{5,4},{6,7},{7,6},{8,9},{9,8},{10,11... | collective-permute-start | bytes 98312 | tf_op jit(solution)/shard_map/ppermute | solution.py:24
  1.1 0.1 collective-permute-start.1
  1.2 0.8 %pad_maximum_fusion.1.tangent_ref = f32[128,128]{1,0:T(8,128)S(1)} fusion(f32[64,128]{1,0:T(8,128)} %param.4, f32[64,128]{1,0:T(8,128)} %param.3), kind=kLoop, calls=%fused_computation.1 | loop fusion | flops 16384 | bytes 131072 | tf_op jit(solution)/shard_map/concatenate | solution.py:195
  2.0 0.2 collective-permute-done
  2.2 0.3 %collective-permute-done.1 = f32[64,128]{1,0:T(8,128)S(1)} collective-permute-done((f32[64,128]{1,0:T(8,128)}, f32[64,128]{1,0:T(8,128)S(1)}, u32[]{:S(2)}, u32[]{:S(2)}) %collective-permute-start.1) | collective-permute-done | bytes 32800 | tf_op jit(solution)/shard_map/ppermute | solution.py:24
  2.6 0.2 collective-permute-start.2
  2.8 2.8 %collective-permute-start.3 = (f32[256,128]{1,0:T(8,128)S(1)}, f32[256,128]{1,0:T(8,128)S(1)}, u32[]{:S(2)}, u32[]{:S(2)}) collective-permute-start(f32[256,128]{1,0:T(8,128)S(1)} %pad_maximum_fusion.chip_ref.refs_5_), channel_id=1, source_target_pairs={{0,2},{1,13},{2,0},{3,15},{4,6},{5,9},{6,4},{7,11},{8,10},{9,5},{1... | collective-permute-start | bytes 393224 | tf_op jit(solution)/shard_map/ppermute | solution.py:24
  5.6 1.6 %collective-permute-start.4 = (f32[256,128]{1,0:T(8,128)S(1)}, f32[256,128]{1,0:T(8,128)S(1)}, u32[]{:S(2)}, u32[]{:S(2)}) collective-permute-start(f32[256,128]{1,0:T(8,128)S(1)} %pad_maximum_fusion.chip_ref.refs_5_), channel_id=1, source_target_pairs={{0,4},{1,9},{2,6},{3,11},{4,0},{5,13},{6,2},{7,15},{8,12},{9,1},{1... | collective-permute-start | bytes 393224 | tf_op jit(solution)/shard_map/ppermute | solution.py:24
  7.2 0.0 collective-permute-done.2.other_counts_ref.refs_4_
  7.2 0.0 copy-start
  7.2 1.2 %copy-done = s32[128,2048]{1,0:T(8,128)S(1)} copy-done((s32[128,2048]{1,0:T(8,128)S(1)}, s32[128,2048]{1,0:T(8,128)}, u32[]{:S(2)}) %copy-start) | copy-done | bytes 1048600
  8.4 0.0 copy-start.1
  8.5 0.2 row_operands.1
  8.6 0.0 collective-permute-done.3.refs_5_
  8.7 2.0 %collective-permute-start.6 = (f32[256,128]{1,0:T(8,128)S(1)}, f32[256,128]{1,0:T(8,128)S(1)}, u32[]{:S(2)}, u32[]{:S(2)}) collective-permute-start(f32[256,128]{1,0:T(8,128)S(1)} %collective-permute-done.3.refs_5_), channel_id=1, source_target_pairs={{0,4},{1,3},{2,6},{3,1},{4,0},{5,7},{6,2},{7,5},{8,12},{9,11},{10,... | collective-permute-start | bytes 393224 | tf_op jit(solution)/shard_map/ppermute | solution.py:24
  10.7 1.0 %collective-permute-done.4.refs_6_ = f32[256,128]{1,0:T(8,128)S(1)} collective-permute-done((f32[256,128]{1,0:T(8,128)S(1)}, f32[256,128]{1,0:T(8,128)S(1)}, u32[]{:S(2)}, u32[]{:S(2)}) %collective-permute-start.4) | collective-permute-done | bytes 131104 | tf_op jit(solution)/shard_map/ppermute | solution.py:24
  11.7 1.8 %collective-permute-start.5 = (f32[256,128]{1,0:T(8,128)S(1)}, f32[256,128]{1,0:T(8,128)S(1)}, u32[]{:S(2)}, u32[]{:S(2)}) collective-permute-start(f32[256,128]{1,0:T(8,128)S(1)} %collective-permute-done.4.refs_6_), channel_id=1, source_target_pairs={{0,1},{1,2},{2,3},{3,0},{4,5},{5,6},{6,7},{7,4},{8,9},{9,10},{10,1... | collective-permute-start | bytes 393224 | tf_op jit(solution)/shard_map/ppermute | solution.py:24
  13.5 0.0 copy-done.1
  13.5 1.1 %chips_0_1.1.refs_6_ = f32[64,512]{1,0:T(8,128)S(1)} custom-call(bf16[512,256]{1,0:T(8,128)(2,1)S(1)} %get-tuple-element.22.refs_0_, bf16[512,256]{1,0:T(8,128)(2,1)S(1)} %get-tuple-element.23.refs_1_, bf16[256,128]{1,0:T(8,128)(2,1)S(1)} %get-tuple-element.24.refs_2_, s32[128,2048]{1,0:T(8,128)S(1)} %copy-done.1, ...), custom_call_target="tpu_custom_call" | custom-call | tf_op jit(solution)/shard_map/chips_0_1/pallas_call | solution.py:182
  14.6 0.4 %collective-permute-done.6.refs_5_ = f32[256,128]{1,0:T(8,128)S(1)} collective-permute-done((f32[256,128]{1,0:T(8,128)S(1)}, f32[256,128]{1,0:T(8,128)S(1)}, u32[]{:S(2)}, u32[]{:S(2)}) %collective-permute-start.6) | collective-permute-done | bytes 131104 | tf_op jit(solution)/shard_map/ppermute | solution.py:24
  14.9 0.6 %chips_2.1.refs_7_ = f32[64,512]{1,0:T(8,128)S(1)} custom-call(bf16[512,256]{1,0:T(8,128)(2,1)S(1)} %get-tuple-element.22.refs_0_, bf16[512,256]{1,0:T(8,128)(2,1)S(1)} %get-tuple-element.23.refs_1_, bf16[256,128]{1,0:T(8,128)(2,1)S(1)} %get-tuple-element.24.refs_2_, s32[128,2048]{1,0:T(8,128)S(1)} %copy-done.1, ...), custom_call_target="tpu_custom_call" | custom-call | tf_op jit(solution)/shard_map/chips_2/pallas_call | solution.py:182
  15.6 1.6 %collective-permute-done.5.refs_6_ = f32[256,128]{1,0:T(8,128)S(1)} collective-permute-done((f32[256,128]{1,0:T(8,128)S(1)}, f32[256,128]{1,0:T(8,128)S(1)}, u32[]{:S(2)}, u32[]{:S(2)}) %collective-permute-start.5) | collective-permute-done | bytes 131104 | tf_op jit(solution)/shard_map/ppermute | solution.py:24
  17.2 0.6 %chips_3.1 = (f32[64,256]{1,0:T(8,128)S(1)}, f32[64,256]{1,0:T(8,128)S(1)}) custom-call(bf16[512,256]{1,0:T(8,128)(2,1)S(1)} %get-tuple-element.22.refs_0_, bf16[512,256]{1,0:T(8,128)(2,1)S(1)} %get-tuple-element.23.refs_1_, bf16[256,128]{1,0:T(8,128)(2,1)S(1)} %get-tuple-element.24.refs_2_, s32[128,2048]{1,0:T(8,128)S(1)} %copy-done.1, ...), custom_call_target="tpu_custom_call" | custom-call | tf_op jit(solution)/shard_map/chips_3/pallas_call | solution.py:182
  17.8 0.1 collective-permute-start.7
  17.9 1.2 %collective-permute-done.7.got_ref = f32[64,256]{1,0:T(8,128)S(1)} collective-permute-done((f32[64,256]{1,0:T(8,128)S(1)}, f32[64,256]{1,0:T(8,128)S(1)}, u32[]{:S(2)}, u32[]{:S(2)}) %collective-permute-start.7) | collective-permute-done | bytes 65568 | tf_op jit(solution)/shard_map/ppermute | solution.py:24
  19.2 0.6 %finish.1 = (f32[64,128]{1,0:T(8,128)}, f32[64,128]{1,0:T(8,128)}, f32[1,128]{1,0:T(1,128)S(1)}) custom-call(f32[128,128]{1,0:T(8,128)S(1)} %pad_maximum_fusion.1.tangent_ref, f32[64,256]{1,0:T(8,128)S(1)} %get-tuple-element.26.mine_ref, f32[64,256]{1,0:T(8,128)S(1)} %collective-permute-done.7.got_ref), custom_call_target="tpu_custom_call" | custom-call | tf_op jit(solution)/shard_map/finish/pallas_call | solution.py:182
  19.8 8.5 %all_to_all.5 = f32[16,1,128]{2,1,0:T(1,128)S(1)} all-to-all(f32[16,1,128]{2,1,0:T(1,128)S(1)} %broadcast_in_dim.9), channel_id=1, replica_groups={{15,14,13,12,11,10,9,8,7,6,5,4,3,2,1,0},{31,30,29,28,27,26,25,24,23,22,..., dimensions={0} | all-to-all | bytes 16384 | tf_op jit(solution)/shard_map/all_to_all | solution.py:268
  28.3 0.5 %slice_bitcast_fusion = f32[2]{0:T(128)} fusion(f32[1,128]{1,0:T(1,128)S(1)} %bitcast.7), kind=kLoop, calls=%fused_computation.2 | loop fusion | bytes 16 | tf_op jit(solution)/shard_map/squeeze | solution.py:269
  (3 shorter events, 0.0 us)
Async XLA Ops:
  0.6 1.6 %collective-permute-start = (f32[64,128]{1,0:T(8,128)}, f32[64,128]{1,0:T(8,128)S(1)}, u32[]{:S(2)}, u32[]{:S(2)}) collective-permute-start(f32[64,128]{1,0:T(8,128)} %param.3), channel_id=1, source_target_pairs={{0,1},{1,0},{2,3},{3,2},{4,5},{5,4},{6,7},{7,6},{8,9},{9,8},{10,11... | collective-permute-start | bytes 98312 | tf_op jit(solution)/shard_map/ppermute | solution.py:24
  1.1 1.4 %collective-permute-start.1 = (f32[64,128]{1,0:T(8,128)}, f32[64,128]{1,0:T(8,128)S(1)}, u32[]{:S(2)}, u32[]{:S(2)}) collective-permute-start(f32[64,128]{1,0:T(8,128)} %param.4), channel_id=1, source_target_pairs={{0,1},{1,0},{2,3},{3,2},{4,5},{5,4},{6,7},{7,6},{8,9},{9,8},{10,11... | collective-permute-start | bytes 98312 | tf_op jit(solution)/shard_map/ppermute | solution.py:24
  2.6 4.6 %collective-permute-start.2 = (s32[128,2048]{1,0:T(8,128)}, s32[128,2048]{1,0:T(8,128)S(1)}, u32[]{:S(2)}, u32[]{:S(2)}) collective-permute-start(s32[128,2048]{1,0:T(8,128)} %refs_3_.2), channel_id=1, source_target_pairs={{0,1},{1,0},{2,3},{3,2},{4,5},{5,4},{6,7},{7,6},{8,9},{9,8},{10,11... | collective-permute-start | bytes 3145736 | tf_op jit(solution)/shard_map/ppermute | solution.py:24
  2.8 5.8 %collective-permute-start.3 = (f32[256,128]{1,0:T(8,128)S(1)}, f32[256,128]{1,0:T(8,128)S(1)}, u32[]{:S(2)}, u32[]{:S(2)}) collective-permute-start(f32[256,128]{1,0:T(8,128)S(1)} %pad_maximum_fusion.chip_ref.refs_5_), channel_id=1, source_target_pairs={{0,2},{1,13},{2,0},{3,15},{4,6},{5,9},{6,4},{7,11},{8,10},{9,5},{1... | collective-permute-start | bytes 393224 | tf_op jit(solution)/shard_map/ppermute | solution.py:24
  5.6 6.0 %collective-permute-start.4 = (f32[256,128]{1,0:T(8,128)S(1)}, f32[256,128]{1,0:T(8,128)S(1)}, u32[]{:S(2)}, u32[]{:S(2)}) collective-permute-start(f32[256,128]{1,0:T(8,128)S(1)} %pad_maximum_fusion.chip_ref.refs_5_), channel_id=1, source_target_pairs={{0,4},{1,9},{2,6},{3,11},{4,0},{5,13},{6,2},{7,15},{8,12},{9,1},{1... | collective-permute-start | bytes 393224 | tf_op jit(solution)/shard_map/ppermute | solution.py:24
  7.2 1.2 %copy-start = (s32[128,2048]{1,0:T(8,128)S(1)}, s32[128,2048]{1,0:T(8,128)}, u32[]{:S(2)}) copy-start(s32[128,2048]{1,0:T(8,128)} %refs_3_.2) | copy-start | bytes 3145732
  8.4 5.0 %copy-start.1 = (s32[128,2048]{1,0:T(8,128)S(1)}, s32[128,2048]{1,0:T(8,128)}, u32[]{:S(2)}) copy-start(s32[128,2048]{1,0:T(8,128)} %refs_3_.2) | copy-start | bytes 3145732
  8.7 6.3 %collective-permute-start.6 = (f32[256,128]{1,0:T(8,128)S(1)}, f32[256,128]{1,0:T(8,128)S(1)}, u32[]{:S(2)}, u32[]{:S(2)}) collective-permute-start(f32[256,128]{1,0:T(8,128)S(1)} %collective-permute-done.3.refs_5_), channel_id=1, source_target_pairs={{0,4},{1,3},{2,6},{3,1},{4,0},{5,7},{6,2},{7,5},{8,12},{9,11},{10,... | collective-permute-start | bytes 393224 | tf_op jit(solution)/shard_map/ppermute | solution.py:24
  11.7 5.5 %collective-permute-start.5 = (f32[256,128]{1,0:T(8,128)S(1)}, f32[256,128]{1,0:T(8,128)S(1)}, u32[]{:S(2)}, u32[]{:S(2)}) collective-permute-start(f32[256,128]{1,0:T(8,128)S(1)} %collective-permute-done.4.refs_6_), channel_id=1, source_target_pairs={{0,1},{1,2},{2,3},{3,0},{4,5},{5,6},{6,7},{7,4},{8,9},{9,10},{10,1... | collective-permute-start | bytes 393224 | tf_op jit(solution)/shard_map/ppermute | solution.py:24
  17.8 1.3 %collective-permute-start.7 = (f32[64,256]{1,0:T(8,128)S(1)}, f32[64,256]{1,0:T(8,128)S(1)}, u32[]{:S(2)}, u32[]{:S(2)}) collective-permute-start(f32[64,256]{1,0:T(8,128)S(1)} %get-tuple-element.27), channel_id=1, source_target_pairs={{0,1},{1,0},{2,3},{3,2},{4,5},{5,4},{6,7},{7,6},{8,9},{9,8},{10,11... | collective-permute-start | bytes 196616 | tf_op jit(solution)/shard_map/ppermute | solution.py:24

commit v3 on v2

--- a/solution.py
+++ b/solution.py
@@ -48,12 +48,12 @@
     half = blks // 2
     if (blks, chips) == (4, 2):
         ops = [
-            (None, (3, 0, 0), (0, 1, 0)),
-            (None, (2, 0, 0), (1, 0, 0)),
-            (0, (0, 1, 0), (1, 0, 0)),
-            (1, (0, 1, 1), (0, 0, 1)),
+            (None, (2, 0, 0), (0, 1, 0)),
+            (None, (3, 1, 1), (1, 0, 1)),
+            (0, (1, 0, 1), (0, 0, 1)),
+            (0, (0, 1, 1), (1, 0, 1)),
         ]
-        return ops, [(0, 0), (1, 1), (2, 2), (None, 3)], [[0, 1], [2], [3]]
+        return ops, [(None, 0), (0, 1), (1, 2), (3, 3)], [[0], [1], [2], [3]]
     ops, slots = [], []
     far = [(b, x) for x in range(chips) for b in range(half, blks)]
     near = [(b, x) for x in range(chips) for b in range(half)][1:] + far[-1:]
@@ -70,7 +70,9 @@
     return ops, slots, [range(half), range(half, len(far) - 1), [len(far) - 1]]
 
 
-def left_kernel(rank, chip_ref, counts_ref, other_counts_ref, first_ref, second_ref, third_ref):
+def left_kernel(
+    rank, places, chip_ref, counts_ref, other_ref, first_ref, second_ref, third_ref, tiles_ref
+):
     span = 2 * rank
     nodes = jnp.concatenate([chip_ref[:span].T, chip_ref[span:].T], 0)
     uh, um, ul = split3(nodes[:, :rank])
@@ -83,9 +85,11 @@
         [jnp.concatenate([um, um, none, none], 1), jnp.concatenate([vm, vm, um, um], 1)], 0
     )
     third_ref[...] = jnp.concatenate([ul, uh], 1)
-
-
-def chip_terms(left, chip, tile_counts, rank, diagonal):
+    for k, place in enumerate(places()):
+        tiles_ref[k] = tile_of(counts_ref, other_ref, place).astype(F32)
+
+
+def chip_terms(left, chip, counted, rank, diagonal):
     first, second, third = left
     rows = third.shape[0]
     span = 2 * rank
@@ -101,7 +105,6 @@
         jnp.concatenate([first[rows:], second[rows:]], 1), jnp.concatenate([right, right], 0)
     )
     rate = jnp.exp(eta)
-    counted = tile_counts.astype(F32)
     if diagonal is not None:
         at_row = lax.broadcasted_iota(jnp.int32, rate.shape, 0)
         at_col = lax.broadcasted_iota(jnp.int32, rate.shape, 1)
@@ -118,34 +121,33 @@
 
 def tile_of(counts_ref, other_counts_ref, place):
     rows = counts_ref.shape[0]
-    chip, me = place
+    chip, first = place
     lines = []
     for ref in (counts_ref, other_counts_ref):
         halves = [
             ref[:, pl.ds(pl.multiple_of((chip * CORES + half) * rows, rows), rows)]
-            for half in (me, 1 - me)
+            for half in (first, 1 - first)
         ]
         lines.append(jnp.concatenate(halves, 1))
     return jnp.concatenate(lines, 0)
 
 
-def chips_kernel(rank, places, is_far, plan, part, *refs):
+def chips_kernel(rank, is_far, plan, part, slot, *refs):
     left = [ref[...] for ref in refs[:3]]
-    counts_ref, other_ref = refs[3:5]
+    tiles_ref = refs[3]
     count = 1 + max(max(entry[:2]) for entry in plan)
-    blocks = refs[5 : 5 + count]
-    rest = refs[5 + count :]
-    rows = counts_ref.shape[0]
+    blocks = refs[4 : 4 + count]
+    rest = refs[4 + count :]
+    rows = tiles_ref.shape[1] // CORES
     outs = 2 if part else 1
     total = rest[0][...] if len(rest) > outs else None
     far = is_far()
-    for (at_far, at_near, is_own), place in zip(plan, places()):
+    for k, (at_far, at_near, is_own) in enumerate(plan):
         chip = blocks[at_far][...]
         if at_far != at_near:
             chip = jnp.where(far, chip, blocks[at_near][...])
-        tile = tile_of(counts_ref, other_ref, place)
         own_core = {FAR: far, NEAR: jnp.logical_not(far), None: None}[is_own]
-        terms = chip_terms(left, chip, tile, rank, own_core)
+        terms = chip_terms(left, chip, tiles_ref[slot + k], rank, own_core)
         total = terms if total is None else total + terms
     if part:
         mine_ref, theirs_ref = rest[-2:]
@@ -155,16 +157,24 @@
         rest[-1][...] = total
 
 
-def finish_kernel(rank, scale, tangent_ref, mine_ref, got_ref, hess_ref, resid_ref, inner_ref):
-    rows = tangent_ref.shape[1]
+def finish_kernel(rank, scale, own_ref, mine_ref, got_ref, total_ref, inner_ref):
+    rows = own_ref.shape[1]
     total = (mine_ref[...] + got_ref[...]) * scale
+    total_ref[...] = total
     hess, resid = total[:, :rows], total[:, rows:]
-    hess_ref[...] = hess
-    resid_ref[...] = resid
     sum_sq = jnp.sum(resid * resid)
-    sum_curv = jnp.sum(tangent_ref[rank:] * hess)
+    sum_curv = jnp.sum(own_ref[rank:] * hess)
     lane = lax.broadcasted_iota(jnp.int32, inner_ref.shape, 1)
     inner_ref[...] = jnp.where(lane == 0, sum_sq, jnp.where(lane == 1, sum_curv, 0.0))
+
+
+def out_kernel(total_ref, parts_ref, hess_ref, resid_ref, inner_ref):
+    rows = hess_ref.shape[1]
+    hess_ref[...] = total_ref[:, :rows]
+    resid_ref[...] = total_ref[:, rows:]
+    inner = jnp.sum(parts_ref[...], 0)
+    for k in range(2):
+        inner_ref[k] = jnp.sum(inner[:, k : k + 1])
 
 
 def local(factors, tangent, counts):
@@ -172,11 +182,11 @@
     nodes = counts.shape[1]
     blks, grps = lax.axis_size("blk"), lax.axis_size("grp")
     chips = grps // CORES
+    vmem = pl.BlockSpec(memory_space=pltpu.VMEM)
+    params = pltpu.CompilerParams(vmem_limit_bytes=40 * 1024 * 1024)
+
     def is_far():
         return lax.axis_index("grp") % CORES == FAR
-
-    vmem = pl.BlockSpec(memory_space=pltpu.VMEM)
-    params = pltpu.CompilerParams(vmem_limit_bytes=40 * 1024 * 1024)
 
     def call(kernel, name, out_shape, *args):
         return pl.pallas_call(
@@ -191,82 +201,95 @@
     def shape(*dims, dtype=F32):
         return jax.ShapeDtypeStruct(dims, dtype)
 
-    swap_cores = functools.partial(permute, blks=blks, chips=chips, moves=[(0, 0, 1)] * 2)
+    swap_cores = functools.partial(permute, blks=blks, chips=chips, moves=[(0, 0, 1)] * CORES)
     own = lax.optimization_barrier(jnp.concatenate([factors, tangent], 0))
     chip = jnp.concatenate([own, swap_cores(factors), swap_cores(tangent)], 0)
     (chip, counts) = lax.optimization_barrier((chip, counts))
-    other_counts = swap_cores(counts)
-
-    ops, slots, groups = schedule(blks, chips)
-    left = call(
-        functools.partial(left_kernel, rank),
-        "row_operands",
-        tuple(
-            shape(n * rows, k * rank, dtype=BF16) for n, k in ((4, 4), (4, 4), (2, 2))
-        ),
-        chip,
-        counts,
-        other_counts,
-    )
-    got, holds = {None: chip}, {None: {FAR: (0, 0, FAR), NEAR: (0, 0, NEAR)}}
-    for k, (src, far_move, near_move) in enumerate(ops):
-        if k == 2:
-            (left, got[src]) = lax.optimization_barrier((left, got[src]))
-        sent = {FAR: far_move, NEAR: near_move}
-        got[k] = permute(got[src], blks, chips, [sent[core] for core in range(CORES)])
+
+    permutes, slots, groups = schedule(blks, chips)
+    holds = {None: {FAR: (0, 0, FAR), NEAR: (0, 0, NEAR)}}
+    for k, (src, *moves) in enumerate(permutes):
+        sent = dict(zip((FAR, NEAR), moves))
         holds[k] = {}
         for core in (FAR, NEAR):
             sender = core ^ sent[core][2]
             b, x, first = holds[src][sender]
             holds[k][core] = (b ^ sent[sender][0], x ^ sent[sender][1], first)
 
-    def places(entries):
+    def places():
         b, g = lax.axis_index("blk"), lax.axis_index("grp")
         far, x = is_far(), g // CORES
         found = []
-        for at_far, at_near in entries:
+        for at_far, at_near in slots:
             ours, theirs = holds[at_far][FAR], holds[at_near][NEAR]
             step_b, step_x, first = (jnp.where(far, p, q) for p, q in zip(ours, theirs))
             found.append(((b ^ step_b) * chips + (x ^ step_x), first))
         return found
 
+    *left, tiles = call(
+        functools.partial(left_kernel, rank, places),
+        "row_operands",
+        (
+            shape(4 * rows, 4 * rank, dtype=BF16),
+            shape(4 * rows, 4 * rank, dtype=BF16),
+            shape(2 * rows, 2 * rank, dtype=BF16),
+            shape(len(slots), 2 * rows, 2 * rows),
+        ),
+        chip,
+        counts,
+        swap_cores(counts),
+    )
+    got = {None: chip}
+    for k, (src, *moves) in enumerate(permutes):
+        sent = dict(zip((FAR, NEAR), moves))
+        if src is not None and permutes[k - 1][0] is None:
+            (left, tiles, got[src]) = lax.optimization_barrier((left, tiles, got[src]))
+        got[k] = permute(got[src], blks, chips, [sent[core] for core in range(CORES)])
+
     total = ()
     for group in groups:
         entries = [slots[k] for k in group]
-        used = []
-        for entry in entries:
-            used += [k for k in dict.fromkeys(entry) if k not in used]
+        used = list(dict.fromkeys(k for entry in entries for k in entry))
         plan = [
             (used.index(p), used.index(q), FAR if p is None else NEAR if q is None else None)
             for p, q in entries
         ]
         part = group is groups[-1]
         total = call(
-            functools.partial(
-                chips_kernel, rank, functools.partial(places, entries), is_far, plan, part
-            ),
-            "chips_" + "_".join(map(str, group)),
+            functools.partial(chips_kernel, rank, is_far, plan, part, group[0]),
+            "chips_%d" % group[0],
             (shape(rank, 2 * rows),) * 2 if part else (shape(rank, 4 * rows),),
             *left,
-            counts,
-            other_counts,
+            tiles,
             *[got[k] for k in used],
             *total,
         )
     mine, theirs = total
-    hess_vec, residual, inner = call(
+    total, inner = call(
         functools.partial(finish_kernel, rank, 1.0 / nodes**0.5),
         "finish",
-        (shape(rank, rows), shape(rank, rows), shape(1, 128)),
+        (shape(rank, 2 * rows), shape(1, 128)),
         own,
         mine,
         swap_cores(theirs),
     )
+
     size = blks * grps
-    spread = jnp.broadcast_to(inner[None], (size, 1, 128))
-    order = [list(range(size))[::-1]]
-    inner = lax.all_to_all(spread, AXES, 0, 0, axis_index_groups=order, tiled=True).sum(0)
-    return hess_vec, residual, inner[0, :2]
+    parts = lax.all_to_all(
+        jnp.broadcast_to(inner[None], (size, 1, 128)),
+        AXES,
+        0,
+        0,
+        axis_index_groups=[list(range(size))[::-1]],
+        tiled=True,
+    )
+    return pl.pallas_call(
+        out_kernel,
+        out_shape=(shape(rank, rows), shape(rank, rows), shape(2)),
+        in_specs=[vmem] * 2,
+        out_specs=(vmem, vmem, pl.BlockSpec(memory_space=pltpu.SMEM)),
+        name="results",
+    )(*(pltpu.with_memory_space_constraint(a, pltpu.VMEM) for a in (total, parts)))
 
 
 def solution(mesh):

time: 29.1 us -> 27.1 us (0.931)
  starting transfers between devices: 9.13 us -> 8.09 us
  waiting for transfers between devices: 4.8 us -> 4.21 us
  local copies, waits for them, and re-layouts: 1.75 us -> 1.23 us
  Pallas kernels: 3.15 us -> 3.52 us
    ppermute x8, starting transfers between devices: 9.13 us -> 8.09 us  [permute(): return lax.ppermute(x, AXES, pairs)]
    pallas_call x0 -> x1, Pallas kernels: none -> 0.68 us  [local(): pl.pallas_call(out_kernel, out_shape=(shape(rank, rows), shape(rank, rows...]
    ppermute x8, waiting for transfers between devices: 4.8 us -> 4.21 us  [permute(): return lax.ppermute(x, AXES, pairs)]
    squeeze x1 -> x0, local copies, waits for them, and re-layouts: 0.51 us -> none  [local(): return (hess_vec, residual, inner[0, :2])]
    pallas_call x5 -> x6, Pallas kernels: 3.15 us -> 2.85 us  [call(): pl.pallas_call(kernel, out_shape=out_shape, in_specs=[vmem] * len(args),...]
    unnamed x4 -> x2, local copies, waits for them, and re-layouts: 1.23 us -> 1.23 us
  transfers between devices with their start and end apart: 8 -> 8, of which waited for: 6 -> 5; matrix products, arithmetic and copies ran while one was open for 3% -> 3% of each run, Pallas kernels for 7% -> 8%
where the time goes in v3:
time: 27.1 us; the launch traced here: 26.9 us
  blocking collectives  8.31 us (31%)
  starting transfers between devices  8.09 us (30%)
  waiting for transfers between devices  4.21 us (16%)
  Pallas kernels  3.52 us (13%)
  local copies, waits for them, and re-layouts  1.23 us (5%)
  other arithmetic  0.79 us (3%)
  between operations  0.71 us (3%)
    all_to_all x1, blocking collectives, local(): lax.all_to_all(jnp.broadcast_to(inner[None], (size, 1, 128)), AXES, 0, 0,...  8.31 us
    ppermute x8, starting transfers between devices, permute(): return lax.ppermute(x, AXES, pairs)  8.09 us
    ppermute x8, waiting for transfers between devices, permute(): return lax.ppermute(x, AXES, pairs)  4.21 us
    pallas_call x6, Pallas kernels, call(): pl.pallas_call(kernel, out_shape=out_shape, in_specs=[vmem] * len(args),...  2.85 us
    unnamed x2, local copies, waits for them, and re-layouts  1.23 us
    concatenate x1, other arithmetic, local(): own = lax.optimization_barrier(jnp.concatenate([factors, tangent], 0))  0.78 us
    pallas_call x1, Pallas kernels, local(): pl.pallas_call(out_kernel, out_shape=(shape(rank, rows), shape(rank, rows...  0.68 us
  transfers between devices with their start and end apart: 8, of which 5 were waited for; matrix products, arithmetic and copies ran while one was open for 3% of the time, Pallas kernels for 8%

profile of v3, /device:TPU:0, one launch (start us, length us, event | category | flops | bytes accessed | tf_op | source)
XLA Modules:
  0.0 26.9 jit_solution(8963680473031610430)
XLA Ops:
  0.6 0.5 %collective-permute-start = (f32[64,128]{1,0:T(8,128)}, f32[64,128]{1,0:T(8,128)S(1)}, u32[]{:S(2)}, u32[]{:S(2)}) collective-permute-start(f32[64,128]{1,0:T(8,128)} %param.3), channel_id=1, source_target_pairs={{0,1},{1,0},{2,3},{3,2},{4,5},{5,4},{6,7},{7,6},{8,9},{9,8},{10,11... | collective-permute-start | bytes 98312 | tf_op jit(solution)/shard_map/ppermute | solution.py:24
  1.1 0.1 collective-permute-start.1
  1.2 0.8 %pad_maximum_fusion.1.own_ref = f32[128,128]{1,0:T(8,128)S(1)} fusion(f32[64,128]{1,0:T(8,128)} %param.4, f32[64,128]{1,0:T(8,128)} %param.3), kind=kLoop, calls=%fused_computation.1 | loop fusion | flops 16384 | bytes 131072 | tf_op jit(solution)/shard_map/concatenate | solution.py:205
  2.0 0.2 collective-permute-done
  2.2 0.3 %collective-permute-done.1 = f32[64,128]{1,0:T(8,128)S(1)} collective-permute-done((f32[64,128]{1,0:T(8,128)}, f32[64,128]{1,0:T(8,128)S(1)}, u32[]{:S(2)}, u32[]{:S(2)}) %collective-permute-start.1) | collective-permute-done | bytes 32800 | tf_op jit(solution)/shard_map/ppermute | solution.py:24
  2.6 0.2 collective-permute-start.2
  2.8 2.8 %collective-permute-start.3 = (f32[256,128]{1,0:T(8,128)S(1)}, f32[256,128]{1,0:T(8,128)S(1)}, u32[]{:S(2)}, u32[]{:S(2)}) collective-permute-start(f32[256,128]{1,0:T(8,128)S(1)} %pad_maximum_fusion.chip_ref.refs_4_), channel_id=1, source_target_pairs={{0,2},{1,9},{2,0},{3,11},{4,6},{5,13},{6,4},{7,15},{8,10},{9,1},{1... | collective-permute-start | bytes 393224 | tf_op jit(solution)/shard_map/ppermute | solution.py:24
  5.6 2.2 %collective-permute-start.5 = (f32[256,128]{1,0:T(8,128)S(1)}, f32[256,128]{1,0:T(8,128)S(1)}, u32[]{:S(2)}, u32[]{:S(2)}) collective-permute-start(f32[256,128]{1,0:T(8,128)S(1)} %pad_maximum_fusion.chip_ref.refs_4_), channel_id=1, source_target_pairs={{0,5},{1,14},{2,7},{3,12},{4,1},{5,10},{6,3},{7,8},{8,13},{9,6},{1... | collective-permute-start | bytes 393224 | tf_op jit(solution)/shard_map/ppermute | solution.py:24
  7.8 0.0 collective-permute-done.2.other_ref
  7.8 0.0 copy-start
  7.8 1.2 %copy-done = s32[128,2048]{1,0:T(8,128)S(1)} copy-done((s32[128,2048]{1,0:T(8,128)S(1)}, s32[128,2048]{1,0:T(8,128)}, u32[]{:S(2)}) %copy-start) | copy-done | bytes 1048600
  9.0 0.3 row_operands.1
  9.3 0.0 collective-permute-done.3.refs_5_.refs_4_
  9.3 2.1 %collective-permute-start.6 = (f32[256,128]{1,0:T(8,128)S(1)}, f32[256,128]{1,0:T(8,128)S(1)}, u32[]{:S(2)}, u32[]{:S(2)}) collective-permute-start(f32[256,128]{1,0:T(8,128)S(1)} %collective-permute-done.3.refs_5_.refs_4_), channel_id=1, source_target_pairs={{0,1},{1,4},{2,3},{3,6},{4,5},{5,0},{6,7},{7,2},{8,9},{9,12},{10,1... | collective-permute-start | bytes 393224 | tf_op jit(solution)/shard_map/ppermute | solution.py:24
  11.4 0.0 collective-permute-start.4
  11.4 0.6 %chips_0.1.refs_6_ = f32[64,512]{1,0:T(8,128)S(1)} custom-call(bf16[512,256]{1,0:T(8,128)(2,1)S(1)} %get-tuple-element.24.refs_0_, bf16[512,256]{1,0:T(8,128)(2,1)S(1)} %get-tuple-element.25.refs_1_, bf16[256,128]{1,0:T(8,128)(2,1)S(1)} %get-tuple-element.26.refs_2_, f32[4,256,256]{2,1,0:T(8,128)S(1)} %get-tuple-element.27.refs_3_, ...), custom_call_target="tpu_custom_call" | custom-call | tf_op jit(solution)/shard_map/chips_0/pallas_call | solution.py:192
  12.0 2.1 %collective-permute-done.5.refs_5_.refs_4_ = f32[256,128]{1,0:T(8,128)S(1)} collective-permute-done((f32[256,128]{1,0:T(8,128)S(1)}, f32[256,128]{1,0:T(8,128)S(1)}, u32[]{:S(2)}, u32[]{:S(2)}) %collective-permute-start.5) | collective-permute-done | bytes 131104 | tf_op jit(solution)/shard_map/ppermute | solution.py:24
  14.1 0.6 %chips_1.1.refs_6_ = f32[64,512]{1,0:T(8,128)S(1)} custom-call(bf16[512,256]{1,0:T(8,128)(2,1)S(1)} %get-tuple-element.24.refs_0_, bf16[512,256]{1,0:T(8,128)(2,1)S(1)} %get-tuple-element.25.refs_1_, bf16[256,128]{1,0:T(8,128)(2,1)S(1)} %get-tuple-element.26.refs_2_, f32[4,256,256]{2,1,0:T(8,128)S(1)} %get-tuple-element.27.refs_3_, ...), custom_call_target="tpu_custom_call" | custom-call | tf_op jit(solution)/shard_map/chips_1/pallas_call | solution.py:192
  14.7 0.0 collective-permute-done.6.refs_5_
  14.7 0.6 %chips_2.1.refs_5_ = f32[64,512]{1,0:T(8,128)S(1)} custom-call(bf16[512,256]{1,0:T(8,128)(2,1)S(1)} %get-tuple-element.24.refs_0_, bf16[512,256]{1,0:T(8,128)(2,1)S(1)} %get-tuple-element.25.refs_1_, bf16[256,128]{1,0:T(8,128)(2,1)S(1)} %get-tuple-element.26.refs_2_, f32[4,256,256]{2,1,0:T(8,128)S(1)} %get-tuple-element.27.refs_3_, ...), custom_call_target="tpu_custom_call" | custom-call | tf_op jit(solution)/shard_map/chips_2/pallas_call | solution.py:192
  15.4 0.4 %collective-permute-done.4.refs_4_ = f32[256,128]{1,0:T(8,128)S(1)} collective-permute-done((f32[256,128]{1,0:T(8,128)S(1)}, f32[256,128]{1,0:T(8,128)S(1)}, u32[]{:S(2)}, u32[]{:S(2)}) %collective-permute-start.4) | collective-permute-done | bytes 131104 | tf_op jit(solution)/shard_map/ppermute | solution.py:24
  15.8 0.6 %chips_3.1 = (f32[64,256]{1,0:T(8,128)S(1)}, f32[64,256]{1,0:T(8,128)S(1)}) custom-call(bf16[512,256]{1,0:T(8,128)(2,1)S(1)} %get-tuple-element.24.refs_0_, bf16[512,256]{1,0:T(8,128)(2,1)S(1)} %get-tuple-element.25.refs_1_, bf16[256,128]{1,0:T(8,128)(2,1)S(1)} %get-tuple-element.26.refs_2_, f32[4,256,256]{2,1,0:T(8,128)S(1)} %get-tuple-element.27.refs_3_, ...), custom_call_target="tpu_custom_call" | custom-call | tf_op jit(solution)/shard_map/chips_3/pallas_call | solution.py:192
  16.4 0.2 collective-permute-start.7
  16.6 1.1 %collective-permute-done.7.got_ref = f32[64,256]{1,0:T(8,128)S(1)} collective-permute-done((f32[64,256]{1,0:T(8,128)S(1)}, f32[64,256]{1,0:T(8,128)S(1)}, u32[]{:S(2)}, u32[]{:S(2)}) %collective-permute-start.7) | collective-permute-done | bytes 65568 | tf_op jit(solution)/shard_map/ppermute | solution.py:24
  17.7 0.1 finish.1
  17.9 8.3 %all_to_all.5.parts_ref = f32[16,1,128]{2,1,0:T(1,128)S(1)} all-to-all(f32[16,1,128]{2,1,0:T(1,128)S(1)} %broadcast_in_dim.9), channel_id=1, replica_groups={{15,14,13,12,11,10,9,8,7,6,5,4,3,2,1,0},{31,30,29,28,27,26,25,24,23,22,..., dimensions={0} | all-to-all | bytes 16384 | tf_op jit(solution)/shard_map/all_to_all | solution.py:278
  26.2 0.7 %results.1 = (f32[64,128]{1,0:T(8,128)}, f32[64,128]{1,0:T(8,128)}, f32[2]{0:T(128)}) custom-call(f32[64,256]{1,0:T(8,128)S(1)} %get-tuple-element.31.total_ref, f32[16,1,128]{2,1,0:T(1,128)S(1)} %all_to_all.5.parts_ref), custom_call_target="tpu_custom_call" | custom-call | tf_op jit(solution)/shard_map/results/pallas_call | solution.py:286
  (2 shorter events, 0.0 us)
Async XLA Ops:
  0.6 1.6 %collective-permute-start = (f32[64,128]{1,0:T(8,128)}, f32[64,128]{1,0:T(8,128)S(1)}, u32[]{:S(2)}, u32[]{:S(2)}) collective-permute-start(f32[64,128]{1,0:T(8,128)} %param.3), channel_id=1, source_target_pairs={{0,1},{1,0},{2,3},{3,2},{4,5},{5,4},{6,7},{7,6},{8,9},{9,8},{10,11... | collective-permute-start | bytes 98312 | tf_op jit(solution)/shard_map/ppermute | solution.py:24
  1.1 1.4 %collective-permute-start.1 = (f32[64,128]{1,0:T(8,128)}, f32[64,128]{1,0:T(8,128)S(1)}, u32[]{:S(2)}, u32[]{:S(2)}) collective-permute-start(f32[64,128]{1,0:T(8,128)} %param.4), channel_id=1, source_target_pairs={{0,1},{1,0},{2,3},{3,2},{4,5},{5,4},{6,7},{7,6},{8,9},{9,8},{10,11... | collective-permute-start | bytes 98312 | tf_op jit(solution)/shard_map/ppermute | solution.py:24
  2.6 5.2 %collective-permute-start.2 = (s32[128,2048]{1,0:T(8,128)}, s32[128,2048]{1,0:T(8,128)S(1)}, u32[]{:S(2)}, u32[]{:S(2)}) collective-permute-start(s32[128,2048]{1,0:T(8,128)} %counts_ref), channel_id=1, source_target_pairs={{0,1},{1,0},{2,3},{3,2},{4,5},{5,4},{6,7},{7,6},{8,9},{9,8},{10,11... | collective-permute-start | bytes 3145736 | tf_op jit(solution)/shard_map/ppermute | solution.py:24
  2.8 6.5 %collective-permute-start.3 = (f32[256,128]{1,0:T(8,128)S(1)}, f32[256,128]{1,0:T(8,128)S(1)}, u32[]{:S(2)}, u32[]{:S(2)}) collective-permute-start(f32[256,128]{1,0:T(8,128)S(1)} %pad_maximum_fusion.chip_ref.refs_4_), channel_id=1, source_target_pairs={{0,2},{1,9},{2,0},{3,11},{4,6},{5,13},{6,4},{7,15},{8,10},{9,1},{1... | collective-permute-start | bytes 393224 | tf_op jit(solution)/shard_map/ppermute | solution.py:24
  5.6 8.5 %collective-permute-start.5 = (f32[256,128]{1,0:T(8,128)S(1)}, f32[256,128]{1,0:T(8,128)S(1)}, u32[]{:S(2)}, u32[]{:S(2)}) collective-permute-start(f32[256,128]{1,0:T(8,128)S(1)} %pad_maximum_fusion.chip_ref.refs_4_), channel_id=1, source_target_pairs={{0,5},{1,14},{2,7},{3,12},{4,1},{5,10},{6,3},{7,8},{8,13},{9,6},{1... | collective-permute-start | bytes 393224 | tf_op jit(solution)/shard_map/ppermute | solution.py:24
  7.8 1.2 %copy-start = (s32[128,2048]{1,0:T(8,128)S(1)}, s32[128,2048]{1,0:T(8,128)}, u32[]{:S(2)}) copy-start(s32[128,2048]{1,0:T(8,128)} %counts_ref) | copy-start | bytes 3145732
  9.3 5.4 %collective-permute-start.6 = (f32[256,128]{1,0:T(8,128)S(1)}, f32[256,128]{1,0:T(8,128)S(1)}, u32[]{:S(2)}, u32[]{:S(2)}) collective-permute-start(f32[256,128]{1,0:T(8,128)S(1)} %collective-permute-done.3.refs_5_.refs_4_), channel_id=1, source_target_pairs={{0,1},{1,4},{2,3},{3,6},{4,5},{5,0},{6,7},{7,2},{8,9},{9,12},{10,1... | collective-permute-start | bytes 393224 | tf_op jit(solution)/shard_map/ppermute | solution.py:24
  11.4 4.4 %collective-permute-start.4 = (f32[256,128]{1,0:T(8,128)S(1)}, f32[256,128]{1,0:T(8,128)S(1)}, u32[]{:S(2)}, u32[]{:S(2)}) collective-permute-start(f32[256,128]{1,0:T(8,128)S(1)} %collective-permute-done.3.refs_5_.refs_4_), channel_id=1, source_target_pairs={{0,5},{1,2},{2,7},{3,0},{4,1},{5,6},{6,3},{7,4},{8,13},{9,10},{10,... | collective-permute-start | bytes 393224 | tf_op jit(solution)/shard_map/ppermute | solution.py:24
  16.4 1.3 %collective-permute-start.7 = (f32[64,256]{1,0:T(8,128)S(1)}, f32[64,256]{1,0:T(8,128)S(1)}, u32[]{:S(2)}, u32[]{:S(2)}) collective-permute-start(f32[64,256]{1,0:T(8,128)S(1)} %get-tuple-element.30), channel_id=1, source_target_pairs={{0,1},{1,0},{2,3},{3,2},{4,5},{5,4},{6,7},{7,6},{8,9},{9,8},{10,11... | collective-permute-start | bytes 196616 | tf_op jit(solution)/shard_map/ppermute | solution.py:24

commit v4 on v3

--- a/solution.py
+++ b/solution.py
@@ -53,7 +53,7 @@
             (0, (1, 0, 1), (0, 0, 1)),
             (0, (0, 1, 1), (1, 0, 1)),
         ]
-        return ops, [(None, 0), (0, 1), (1, 2), (3, 3)], [[0], [1], [2], [3]]
+        return ops, [(None, 0), (0, 1), (1, 2), (3, 3)], [[0], [1], [2]]
     ops, slots = [], []
     far = [(b, x) for x in range(chips) for b in range(half, blks)]
     near = [(b, x) for x in range(chips) for b in range(half)][1:] + far[-1:]
@@ -67,46 +67,32 @@
         ops.append((src, far_move, near_move))
         slots.append((k, k))
     slots[-1] = (None, len(far) - 1)
-    return ops, slots, [range(half), range(half, len(far) - 1), [len(far) - 1]]
-
-
-def left_kernel(
-    rank, places, chip_ref, counts_ref, other_ref, first_ref, second_ref, third_ref, tiles_ref
-):
+    groups = [range(half), range(half, len(far) - 1)]
+    return ops, slots, [group for group in groups if group]
+
+
+def left_kernel(rank, places, chip_ref, counts_ref, other_ref, eta_ref, deta_ref, tiles_ref):
     span = 2 * rank
     nodes = jnp.concatenate([chip_ref[:span].T, chip_ref[span:].T], 0)
     uh, um, ul = split3(nodes[:, :rank])
     vh, vm = split2(nodes[:, rank:])
-    none = jnp.zeros_like(uh)
-    first_ref[...] = jnp.concatenate(
-        [jnp.concatenate([uh, uh, none, none], 1), jnp.concatenate([vh, vh, uh, uh], 1)], 0
-    )
-    second_ref[...] = jnp.concatenate(
-        [jnp.concatenate([um, um, none, none], 1), jnp.concatenate([vm, vm, um, um], 1)], 0
-    )
-    third_ref[...] = jnp.concatenate([ul, uh], 1)
+    eta_ref[...] = jnp.concatenate([uh, uh, um, um, ul, uh], 1)
+    deta_ref[...] = jnp.concatenate([vh, vh, uh, uh, vm, vm, um, um], 1)
     for k, place in enumerate(places()):
         tiles_ref[k] = tile_of(counts_ref, other_ref, place).astype(F32)
 
 
-def chip_terms(left, chip, counted, rank, diagonal):
-    first, second, third = left
-    rows = third.shape[0]
+def chip_terms(eta_left, deta_left, chip, counted, rank, diagonal, start=0):
+    rows = eta_left.shape[0]
     span = 2 * rank
     cols = jnp.concatenate([chip[:span], chip[span:]], 1)
     uh, um, ul = split3(cols[:rank])
     vh, vm = split2(cols[rank:])
-    right = jnp.concatenate([uh, um, vh, vm], 0)
-    eta = dot(
-        jnp.concatenate([first[:rows], second[:rows], third], 1),
-        jnp.concatenate([right, right, uh, ul], 0),
-    )
-    deta = dot(
-        jnp.concatenate([first[rows:], second[rows:]], 1), jnp.concatenate([right, right], 0)
-    )
+    eta = dot(eta_left, jnp.concatenate([uh, um, uh, um, uh, ul], 0))
+    deta = dot(deta_left, jnp.concatenate([uh, um, vh, vm, uh, um, vh, vm], 0))
     rate = jnp.exp(eta)
     if diagonal is not None:
-        at_row = lax.broadcasted_iota(jnp.int32, rate.shape, 0)
+        at_row = start + lax.broadcasted_iota(jnp.int32, rate.shape, 0)
         at_col = lax.broadcasted_iota(jnp.int32, rate.shape, 1)
         keep = jnp.logical_or(at_row != at_col, jnp.logical_not(diagonal))
         rate = jnp.where(keep, rate, 0.0)
@@ -132,29 +118,36 @@
     return jnp.concatenate(lines, 0)
 
 
-def chips_kernel(rank, is_far, plan, part, slot, *refs):
-    left = [ref[...] for ref in refs[:3]]
-    tiles_ref = refs[3]
-    count = 1 + max(max(entry[:2]) for entry in plan)
-    blocks = refs[4 : 4 + count]
-    rest = refs[4 + count :]
-    rows = tiles_ref.shape[1] // CORES
-    outs = 2 if part else 1
-    total = rest[0][...] if len(rest) > outs else None
+def pick_chip(far, entry, blocks):
+    at_far, at_near, own_core = entry
+    chip = blocks[at_far][...]
+    if at_far != at_near:
+        chip = jnp.where(far, chip, blocks[at_near][...])
+    return chip, {FAR: far, NEAR: jnp.logical_not(far), None: None}[own_core]
+
+
+def chips_kernel(rank, is_far, plan, slot, count, *refs):
+    eta_ref, deta_ref, tiles_ref = refs[:3]
+    blocks, before = refs[3 : 3 + count], refs[3 + count : -1]
     far = is_far()
-    for k, (at_far, at_near, is_own) in enumerate(plan):
-        chip = blocks[at_far][...]
-        if at_far != at_near:
-            chip = jnp.where(far, chip, blocks[at_near][...])
-        own_core = {FAR: far, NEAR: jnp.logical_not(far), None: None}[is_own]
-        terms = chip_terms(left, chip, tiles_ref[slot + k], rank, own_core)
+    total = before[0][...] if before else None
+    for k, entry in enumerate(plan):
+        chip, own = pick_chip(far, entry, blocks)
+        terms = chip_terms(eta_ref[...], deta_ref[...], chip, tiles_ref[slot + k], rank, own)
         total = terms if total is None else total + terms
-    if part:
-        mine_ref, theirs_ref = rest[-2:]
-        mine_ref[...] = jnp.concatenate([total[:, :rows], total[:, 2 * rows : 3 * rows]], 1)
-        theirs_ref[...] = jnp.concatenate([total[:, rows : 2 * rows], total[:, 3 * rows :]], 1)
-    else:
-        rest[-1][...] = total
+    refs[-1][...] = total
+
+
+def last_kernel(rank, is_far, entry, slot, half, *refs):
+    eta_ref, deta_ref, tiles_ref, *blocks, sum_ref, out_ref = refs
+    rows = eta_ref.shape[0] // CORES
+    mine = slice(half * rows, (half + 1) * rows)
+    chip, own = pick_chip(is_far(), entry, blocks)
+    terms = chip_terms(
+        eta_ref[mine], deta_ref[mine], chip, tiles_ref[slot][mine], rank, own, half * rows
+    )
+    resid = slice((CORES + half) * rows, (CORES + half + 1) * rows)
+    out_ref[...] = terms + jnp.concatenate([sum_ref[:, mine], sum_ref[:, resid]], 1)
 
 
 def finish_kernel(rank, scale, own_ref, mine_ref, got_ref, total_ref, inner_ref):
@@ -230,9 +223,8 @@
         functools.partial(left_kernel, rank, places),
         "row_operands",
         (
-            shape(4 * rows, 4 * rank, dtype=BF16),
-            shape(4 * rows, 4 * rank, dtype=BF16),
-            shape(2 * rows, 2 * rank, dtype=BF16),
+            shape(2 * rows, 6 * rank, dtype=BF16),
+            shape(2 * rows, 8 * rank, dtype=BF16),
             shape(len(slots), 2 * rows, 2 * rows),
         ),
         chip,
@@ -246,25 +238,37 @@
             (left, tiles, got[src]) = lax.optimization_barrier((left, tiles, got[src]))
         got[k] = permute(got[src], blks, chips, [sent[core] for core in range(CORES)])
 
+    def plan_of(entries):
+        used = list(dict.fromkeys(k for entry in entries for k in entry))
+        own = [FAR if p is None else NEAR if q is None else None for p, q in entries]
+        plan = [(used.index(p), used.index(q), o) for (p, q), o in zip(entries, own)]
+        return plan, [got[k] for k in used]
+
     total = ()
     for group in groups:
-        entries = [slots[k] for k in group]
-        used = list(dict.fromkeys(k for entry in entries for k in entry))
-        plan = [
-            (used.index(p), used.index(q), FAR if p is None else NEAR if q is None else None)
-            for p, q in entries
-        ]
-        part = group is groups[-1]
+        plan, blocks = plan_of([slots[k] for k in group])
         total = call(
-            functools.partial(chips_kernel, rank, is_far, plan, part, group[0]),
+            functools.partial(chips_kernel, rank, is_far, plan, group[0], len(blocks)),
             "chips_%d" % group[0],
-            (shape(rank, 2 * rows),) * 2 if part else (shape(rank, 4 * rows),),
+            (shape(rank, 4 * rows),),
             *left,
             tiles,
-            *[got[k] for k in used],
+            *blocks,
             *total,
         )
-    mine, theirs = total
+    plan, blocks = plan_of(slots[-1:])
+    theirs, mine = (
+        call(
+            functools.partial(last_kernel, rank, is_far, plan[0], len(slots) - 1, half),
+            "last_chip_%d" % half,
+            shape(rank, 2 * rows),
+            *left,
+            tiles,
+            *blocks,
+            *total,
+        )
+        for half in (1, 0)
+    )
     total, inner = call(
         functools.partial(finish_kernel, rank, 1.0 / nodes**0.5),
         "finish",

time: 27.1 us -> 27 us (level)
  waiting for transfers between devices: 4.21 us -> 3.89 us
    ppermute x8, waiting for transfers between devices: 4.21 us -> 3.89 us  [permute(): return lax.ppermute(x, AXES, pairs)]
    pallas_call x6 -> x7, Pallas kernels: 2.85 us -> 2.99 us  [call(): pl.pallas_call(kernel, out_shape=out_shape, in_specs=[vmem] * len(args),...]
  transfers between devices with their start and end apart: 8 -> 8, of which waited for: 5 -> 5; matrix products, arithmetic and copies ran while one was open for 3% -> 3% of each run, Pallas kernels for 8% -> 9%
where the time goes in v4:
time: 27 us; the launch traced here: 26.7 us
  blocking collectives  8.31 us (31%)
  starting transfers between devices  8.1 us (30%)
  waiting for transfers between devices  3.89 us (14%)
  Pallas kernels  3.67 us (14%)
  local copies, waits for them, and re-layouts  1.23 us (5%)
  other arithmetic  0.79 us (3%)
  between operations  0.72 us (3%)
    all_to_all x1, blocking collectives, local(): lax.all_to_all(jnp.broadcast_to(inner[None], (size, 1, 128)), AXES, 0, 0,...  8.31 us
    ppermute x8, starting transfers between devices, permute(): return lax.ppermute(x, AXES, pairs)  8.1 us
    ppermute x8, waiting for transfers between devices, permute(): return lax.ppermute(x, AXES, pairs)  3.89 us
    pallas_call x7, Pallas kernels, call(): pl.pallas_call(kernel, out_shape=out_shape, in_specs=[vmem] * len(args),...  2.99 us
    unnamed x2, local copies, waits for them, and re-layouts  1.23 us
    concatenate x1, other arithmetic, local(): own = lax.optimization_barrier(jnp.concatenate([factors, tangent], 0))  0.78 us
    pallas_call x1, Pallas kernels, local(): pl.pallas_call(out_kernel, out_shape=(shape(rank, rows), shape(rank, rows...  0.68 us
  transfers between devices with their start and end apart: 8, of which 5 were waited for; matrix products, arithmetic and copies ran while one was open for 3% of the time, Pallas kernels for 9%

profile of v4, /device:TPU:0, one launch (start us, length us, event | category | flops | bytes accessed | tf_op | source)
XLA Modules:
  0.0 26.7 jit_solution(2206515322694694670)
XLA Ops:
  0.6 0.5 %collective-permute-start = (f32[64,128]{1,0:T(8,128)}, f32[64,128]{1,0:T(8,128)S(1)}, u32[]{:S(2)}, u32[]{:S(2)}) collective-permute-start(f32[64,128]{1,0:T(8,128)} %param.3), channel_id=1, source_target_pairs={{0,1},{1,0},{2,3},{3,2},{4,5},{5,4},{6,7},{7,6},{8,9},{9,8},{10,11... | collective-permute-start | bytes 98312 | tf_op jit(solution)/shard_map/ppermute | solution.py:24
  1.1 0.1 collective-permute-start.1
  1.2 0.8 %pad_maximum_fusion.1.own_ref = f32[128,128]{1,0:T(8,128)S(1)} fusion(f32[64,128]{1,0:T(8,128)} %param.4, f32[64,128]{1,0:T(8,128)} %param.3), kind=kLoop, calls=%fused_computation.1 | loop fusion | flops 16384 | bytes 131072 | tf_op jit(solution)/shard_map/concatenate | solution.py:198
  2.0 0.2 collective-permute-done
  2.2 0.3 %collective-permute-done.1 = f32[64,128]{1,0:T(8,128)S(1)} collective-permute-done((f32[64,128]{1,0:T(8,128)}, f32[64,128]{1,0:T(8,128)S(1)}, u32[]{:S(2)}, u32[]{:S(2)}) %collective-permute-start.1) | collective-permute-done | bytes 32800 | tf_op jit(solution)/shard_map/ppermute | solution.py:24
  2.6 0.2 collective-permute-start.2
  2.8 2.8 %collective-permute-start.3 = (f32[256,128]{1,0:T(8,128)S(1)}, f32[256,128]{1,0:T(8,128)S(1)}, u32[]{:S(2)}, u32[]{:S(2)}) collective-permute-start(f32[256,128]{1,0:T(8,128)S(1)} %pad_maximum_fusion.chip_ref.refs_3_), channel_id=1, source_target_pairs={{0,2},{1,9},{2,0},{3,11},{4,6},{5,13},{6,4},{7,15},{8,10},{9,1},{1... | collective-permute-start | bytes 393224 | tf_op jit(solution)/shard_map/ppermute | solution.py:24
  5.6 2.2 %collective-permute-start.5 = (f32[256,128]{1,0:T(8,128)S(1)}, f32[256,128]{1,0:T(8,128)S(1)}, u32[]{:S(2)}, u32[]{:S(2)}) collective-permute-start(f32[256,128]{1,0:T(8,128)S(1)} %pad_maximum_fusion.chip_ref.refs_3_), channel_id=1, source_target_pairs={{0,5},{1,14},{2,7},{3,12},{4,1},{5,10},{6,3},{7,8},{8,13},{9,6},{1... | collective-permute-start | bytes 393224 | tf_op jit(solution)/shard_map/ppermute | solution.py:24
  7.8 0.0 collective-permute-done.2.other_ref
  7.8 0.0 copy-start
  7.8 1.2 %copy-done = s32[128,2048]{1,0:T(8,128)S(1)} copy-done((s32[128,2048]{1,0:T(8,128)S(1)}, s32[128,2048]{1,0:T(8,128)}, u32[]{:S(2)}) %copy-start) | copy-done | bytes 1048600
  9.0 0.2 row_operands.1
  9.3 0.0 collective-permute-done.3.refs_4_.refs_3_
  9.3 2.1 %collective-permute-start.6 = (f32[256,128]{1,0:T(8,128)S(1)}, f32[256,128]{1,0:T(8,128)S(1)}, u32[]{:S(2)}, u32[]{:S(2)}) collective-permute-start(f32[256,128]{1,0:T(8,128)S(1)} %collective-permute-done.3.refs_4_.refs_3_), channel_id=1, source_target_pairs={{0,1},{1,4},{2,3},{3,6},{4,5},{5,0},{6,7},{7,2},{8,9},{9,12},{10,1... | collective-permute-start | bytes 393224 | tf_op jit(solution)/shard_map/ppermute | solution.py:24
  11.4 0.0 collective-permute-start.4
  11.4 0.6 %chips_0.1.refs_5_ = f32[64,512]{1,0:T(8,128)S(1)} custom-call(bf16[256,384]{1,0:T(8,128)(2,1)S(1)} %get-tuple-element.19.refs_0_, bf16[256,512]{1,0:T(8,128)(2,1)S(1)} %get-tuple-element.20.refs_1_, f32[4,256,256]{2,1,0:T(8,128)S(1)} %get-tuple-element.21.refs_2_, f32[256,128]{1,0:T(8,128)S(1)} %pad_maximum_fusion.chip_ref.refs_3_, ...), custom_call_target="tpu_custom_call" | custom-call | tf_op jit(solution)/shard_map/chips_0/pallas_call | solution.py:185
  12.0 2.1 %collective-permute-done.5.refs_4_.refs_3_ = f32[256,128]{1,0:T(8,128)S(1)} collective-permute-done((f32[256,128]{1,0:T(8,128)S(1)}, f32[256,128]{1,0:T(8,128)S(1)}, u32[]{:S(2)}, u32[]{:S(2)}) %collective-permute-start.5) | collective-permute-done | bytes 131104 | tf_op jit(solution)/shard_map/ppermute | solution.py:24
  14.1 0.6 %chips_1.1.refs_5_ = f32[64,512]{1,0:T(8,128)S(1)} custom-call(bf16[256,384]{1,0:T(8,128)(2,1)S(1)} %get-tuple-element.19.refs_0_, bf16[256,512]{1,0:T(8,128)(2,1)S(1)} %get-tuple-element.20.refs_1_, f32[4,256,256]{2,1,0:T(8,128)S(1)} %get-tuple-element.21.refs_2_, f32[256,128]{1,0:T(8,128)S(1)} %collective-permute-done.3.refs_4_.refs_3_, ...), custom_call_target="tpu_custom_call" | custom-call | tf_op jit(solution)/shard_map/chips_1/pallas_call | solution.py:185
  14.7 0.0 collective-permute-done.6.refs_4_
  14.7 0.6 %chips_2.1.refs_4_ = f32[64,512]{1,0:T(8,128)S(1)} custom-call(bf16[256,384]{1,0:T(8,128)(2,1)S(1)} %get-tuple-element.19.refs_0_, bf16[256,512]{1,0:T(8,128)(2,1)S(1)} %get-tuple-element.20.refs_1_, f32[4,256,256]{2,1,0:T(8,128)S(1)} %get-tuple-element.21.refs_2_, f32[256,128]{1,0:T(8,128)S(1)} %collective-permute-done.5.refs_4_.refs_3_, ...), custom_call_target="tpu_custom_call" | custom-call | tf_op jit(solution)/shard_map/chips_2/pallas_call | solution.py:185
  15.3 0.5 %collective-permute-done.4.refs_3_ = f32[256,128]{1,0:T(8,128)S(1)} collective-permute-done((f32[256,128]{1,0:T(8,128)S(1)}, f32[256,128]{1,0:T(8,128)S(1)}, u32[]{:S(2)}, u32[]{:S(2)}) %collective-permute-start.4) | collective-permute-done | bytes 131104 | tf_op jit(solution)/shard_map/ppermute | solution.py:24
  15.8 0.4 %last_chip_1.1 = f32[64,256]{1,0:T(8,128)S(1)} custom-call(bf16[256,384]{1,0:T(8,128)(2,1)S(1)} %get-tuple-element.19.refs_0_, bf16[256,512]{1,0:T(8,128)(2,1)S(1)} %get-tuple-element.20.refs_1_, f32[4,256,256]{2,1,0:T(8,128)S(1)} %get-tuple-element.21.refs_2_, f32[256,128]{1,0:T(8,128)S(1)} %collective-permute-done.4.refs_3_, f32[64,512]{1,0:T(8,128)S(1)} %chips_2.1.refs_4_), custom_call_target="tpu_custom_call" | custom-call | tf_op jit(solution)/shard_map/last_chip_1/pallas_call | solution.py:185
  16.2 0.2 collective-permute-start.7
  16.4 0.4 %last_chip_0.1.mine_ref = f32[64,256]{1,0:T(8,128)S(1)} custom-call(bf16[256,384]{1,0:T(8,128)(2,1)S(1)} %get-tuple-element.19.refs_0_, bf16[256,512]{1,0:T(8,128)(2,1)S(1)} %get-tuple-element.20.refs_1_, f32[4,256,256]{2,1,0:T(8,128)S(1)} %get-tuple-element.21.refs_2_, f32[256,128]{1,0:T(8,128)S(1)} %collective-permute-done.4.refs_3_, ...), custom_call_target="tpu_custom_call" | custom-call | tf_op jit(solution)/shard_map/last_chip_0/pallas_call | solution.py:185
  16.9 0.7 %collective-permute-done.7.got_ref = f32[64,256]{1,0:T(8,128)S(1)} collective-permute-done((f32[64,256]{1,0:T(8,128)S(1)}, f32[64,256]{1,0:T(8,128)S(1)}, u32[]{:S(2)}, u32[]{:S(2)}) %collective-permute-start.7) | collective-permute-done | bytes 65568 | tf_op jit(solution)/shard_map/ppermute | solution.py:24
  17.6 0.1 finish.1
  17.7 8.3 %all_to_all.5.parts_ref = f32[16,1,128]{2,1,0:T(1,128)S(1)} all-to-all(f32[16,1,128]{2,1,0:T(1,128)S(1)} %broadcast_in_dim.9), channel_id=1, replica_groups={{15,14,13,12,11,10,9,8,7,6,5,4,3,2,1,0},{31,30,29,28,27,26,25,24,23,22,..., dimensions={0} | all-to-all | bytes 16384 | tf_op jit(solution)/shard_map/all_to_all | solution.py:282
  26.0 0.7 %results.1 = (f32[64,128]{1,0:T(8,128)}, f32[64,128]{1,0:T(8,128)}, f32[2]{0:T(128)}) custom-call(f32[64,256]{1,0:T(8,128)S(1)} %get-tuple-element.23.total_ref, f32[16,1,128]{2,1,0:T(1,128)S(1)} %all_to_all.5.parts_ref), custom_call_target="tpu_custom_call" | custom-call | tf_op jit(solution)/shard_map/results/pallas_call | solution.py:290
  (2 shorter events, 0.0 us)
Async XLA Ops:
  0.6 1.6 %collective-permute-start = (f32[64,128]{1,0:T(8,128)}, f32[64,128]{1,0:T(8,128)S(1)}, u32[]{:S(2)}, u32[]{:S(2)}) collective-permute-start(f32[64,128]{1,0:T(8,128)} %param.3), channel_id=1, source_target_pairs={{0,1},{1,0},{2,3},{3,2},{4,5},{5,4},{6,7},{7,6},{8,9},{9,8},{10,11... | collective-permute-start | bytes 98312 | tf_op jit(solution)/shard_map/ppermute | solution.py:24
  1.1 1.4 %collective-permute-start.1 = (f32[64,128]{1,0:T(8,128)}, f32[64,128]{1,0:T(8,128)S(1)}, u32[]{:S(2)}, u32[]{:S(2)}) collective-permute-start(f32[64,128]{1,0:T(8,128)} %param.4), channel_id=1, source_target_pairs={{0,1},{1,0},{2,3},{3,2},{4,5},{5,4},{6,7},{7,6},{8,9},{9,8},{10,11... | collective-permute-start | bytes 98312 | tf_op jit(solution)/shard_map/ppermute | solution.py:24
  2.6 5.2 %collective-permute-start.2 = (s32[128,2048]{1,0:T(8,128)}, s32[128,2048]{1,0:T(8,128)S(1)}, u32[]{:S(2)}, u32[]{:S(2)}) collective-permute-start(s32[128,2048]{1,0:T(8,128)} %counts_ref), channel_id=1, source_target_pairs={{0,1},{1,0},{2,3},{3,2},{4,5},{5,4},{6,7},{7,6},{8,9},{9,8},{10,11... | collective-permute-start | bytes 3145736 | tf_op jit(solution)/shard_map/ppermute | solution.py:24
  2.8 6.5 %collective-permute-start.3 = (f32[256,128]{1,0:T(8,128)S(1)}, f32[256,128]{1,0:T(8,128)S(1)}, u32[]{:S(2)}, u32[]{:S(2)}) collective-permute-start(f32[256,128]{1,0:T(8,128)S(1)} %pad_maximum_fusion.chip_ref.refs_3_), channel_id=1, source_target_pairs={{0,2},{1,9},{2,0},{3,11},{4,6},{5,13},{6,4},{7,15},{8,10},{9,1},{1... | collective-permute-start | bytes 393224 | tf_op jit(solution)/shard_map/ppermute | solution.py:24
  5.6 8.5 %collective-permute-start.5 = (f32[256,128]{1,0:T(8,128)S(1)}, f32[256,128]{1,0:T(8,128)S(1)}, u32[]{:S(2)}, u32[]{:S(2)}) collective-permute-start(f32[256,128]{1,0:T(8,128)S(1)} %pad_maximum_fusion.chip_ref.refs_3_), channel_id=1, source_target_pairs={{0,5},{1,14},{2,7},{3,12},{4,1},{5,10},{6,3},{7,8},{8,13},{9,6},{1... | collective-permute-start | bytes 393224 | tf_op jit(solution)/shard_map/ppermute | solution.py:24
  7.8 1.2 %copy-start = (s32[128,2048]{1,0:T(8,128)S(1)}, s32[128,2048]{1,0:T(8,128)}, u32[]{:S(2)}) copy-start(s32[128,2048]{1,0:T(8,128)} %counts_ref) | copy-start | bytes 3145732
  9.3 5.4 %collective-permute-start.6 = (f32[256,128]{1,0:T(8,128)S(1)}, f32[256,128]{1,0:T(8,128)S(1)}, u32[]{:S(2)}, u32[]{:S(2)}) collective-permute-start(f32[256,128]{1,0:T(8,128)S(1)} %collective-permute-done.3.refs_4_.refs_3_), channel_id=1, source_target_pairs={{0,1},{1,4},{2,3},{3,6},{4,5},{5,0},{6,7},{7,2},{8,9},{9,12},{10,1... | collective-permute-start | bytes 393224 | tf_op jit(solution)/shard_map/ppermute | solution.py:24
  11.4 4.4 %collective-permute-start.4 = (f32[256,128]{1,0:T(8,128)S(1)}, f32[256,128]{1,0:T(8,128)S(1)}, u32[]{:S(2)}, u32[]{:S(2)}) collective-permute-start(f32[256,128]{1,0:T(8,128)S(1)} %collective-permute-done.3.refs_4_.refs_3_), channel_id=1, source_target_pairs={{0,5},{1,2},{2,7},{3,0},{4,1},{5,6},{6,3},{7,4},{8,13},{9,10},{10,... | collective-permute-start | bytes 393224 | tf_op jit(solution)/shard_map/ppermute | solution.py:24
  16.2 1.3 %collective-permute-start.7 = (f32[64,256]{1,0:T(8,128)S(1)}, f32[64,256]{1,0:T(8,128)S(1)}, u32[]{:S(2)}, u32[]{:S(2)}) collective-permute-start(f32[64,256]{1,0:T(8,128)S(1)} %last_chip_1.1), channel_id=1, source_target_pairs={{0,1},{1,0},{2,3},{3,2},{4,5},{5,4},{6,7},{7,6},{8,9},{9,8},{10,11... | collective-permute-start | bytes 196616 | tf_op jit(solution)/shard_map/ppermute | solution.py:24

commit v5 on v4

--- a/solution.py
+++ b/solution.py
@@ -53,7 +53,7 @@
             (0, (1, 0, 1), (0, 0, 1)),
             (0, (0, 1, 1), (1, 0, 1)),
         ]
-        return ops, [(None, 0), (0, 1), (1, 2), (3, 3)], [[0], [1], [2]]
+        return ops, [(None, 0), (0, 1), (1, 2), (3, 3)], [[0], [1, 2]]
     ops, slots = [], []
     far = [(b, x) for x in range(chips) for b in range(half, blks)]
     near = [(b, x) for x in range(chips) for b in range(half)][1:] + far[-1:]
@@ -280,7 +280,9 @@
 
     size = blks * grps
     parts = lax.all_to_all(
-        jnp.broadcast_to(inner[None], (size, 1, 128)),
+        pltpu.with_memory_space_constraint(
+            jnp.broadcast_to(inner[None], (size, 1, 128)), pltpu.VMEM
+        ),
         AXES,
         0,
         0,

time: 27 us -> 27 us (level)
    pallas_call x7 -> x6, Pallas kernels: 2.99 us -> 2.83 us  [call(): pl.pallas_call(kernel, out_shape=out_shape, in_specs=[vmem] * len(args),...]
  transfers between devices with their start and end apart: 8 -> 8, of which waited for: 5 -> 6; matrix products, arithmetic and copies ran while one was open for 3% -> 3% of each run, Pallas kernels for 9% -> 8%
where the time goes in v5:
time: 27 us; the launch traced here: 26.7 us
  blocking collectives  8.33 us (31%)
  starting transfers between devices  8.1 us (30%)
  waiting for transfers between devices  4.07 us (15%)
  Pallas kernels  3.5 us (13%)
  local copies, waits for them, and re-layouts  1.23 us (5%)
  other arithmetic  0.79 us (3%)
  between operations  0.71 us (3%)
    all_to_all x1, blocking collectives, local(): lax.all_to_all(pltpu.with_memory_space_constraint(jnp.broadcast_to(inner[...  8.33 us
    ppermute x8, starting transfers between devices, permute(): return lax.ppermute(x, AXES, pairs)  8.1 us
    ppermute x8, waiting for transfers between devices, permute(): return lax.ppermute(x, AXES, pairs)  4.07 us
    pallas_call x6, Pallas kernels, call(): pl.pallas_call(kernel, out_shape=out_shape, in_specs=[vmem] * len(args),...  2.83 us
    unnamed x2, local copies, waits for them, and re-layouts  1.23 us
    concatenate x1, other arithmetic, local(): own = lax.optimization_barrier(jnp.concatenate([factors, tangent], 0))  0.78 us
    pallas_call x1, Pallas kernels, local(): pl.pallas_call(out_kernel, out_shape=(shape(rank, rows), shape(rank, rows...  0.68 us
  transfers between devices with their start and end apart: 8, of which 6 were waited for; matrix products, arithmetic and copies ran while one was open for 3% of the time, Pallas kernels for 8%

profile of v5, /device:TPU:0, one launch (start us, length us, event | category | flops | bytes accessed | tf_op | source)
XLA Modules:
  0.0 26.7 jit_solution(18140832523844990489)
XLA Ops:
  0.6 0.5 %collective-permute-start = (f32[64,128]{1,0:T(8,128)}, f32[64,128]{1,0:T(8,128)S(1)}, u32[]{:S(2)}, u32[]{:S(2)}) collective-permute-start(f32[64,128]{1,0:T(8,128)} %param.3), channel_id=1, source_target_pairs={{0,1},{1,0},{2,3},{3,2},{4,5},{5,4},{6,7},{7,6},{8,9},{9,8},{10,11... | collective-permute-start | bytes 98312 | tf_op jit(solution)/shard_map/ppermute | solution.py:24
  1.1 0.1 collective-permute-start.1
  1.2 0.8 %pad_maximum_fusion.1.own_ref = f32[128,128]{1,0:T(8,128)S(1)} fusion(f32[64,128]{1,0:T(8,128)} %param.4, f32[64,128]{1,0:T(8,128)} %param.3), kind=kLoop, calls=%fused_computation.1 | loop fusion | flops 16384 | bytes 131072 | tf_op jit(solution)/shard_map/concatenate | solution.py:198
  2.0 0.2 collective-permute-done
  2.2 0.3 %collective-permute-done.1 = f32[64,128]{1,0:T(8,128)S(1)} collective-permute-done((f32[64,128]{1,0:T(8,128)}, f32[64,128]{1,0:T(8,128)S(1)}, u32[]{:S(2)}, u32[]{:S(2)}) %collective-permute-start.1) | collective-permute-done | bytes 32800 | tf_op jit(solution)/shard_map/ppermute | solution.py:24
  2.6 0.2 collective-permute-start.2
  2.8 2.8 %collective-permute-start.3 = (f32[256,128]{1,0:T(8,128)S(1)}, f32[256,128]{1,0:T(8,128)S(1)}, u32[]{:S(2)}, u32[]{:S(2)}) collective-permute-start(f32[256,128]{1,0:T(8,128)S(1)} %pad_maximum_fusion.chip_ref.refs_3_), channel_id=1, source_target_pairs={{0,2},{1,9},{2,0},{3,11},{4,6},{5,13},{6,4},{7,15},{8,10},{9,1},{1... | collective-permute-start | bytes 393224 | tf_op jit(solution)/shard_map/ppermute | solution.py:24
  5.6 2.2 %collective-permute-start.5 = (f32[256,128]{1,0:T(8,128)S(1)}, f32[256,128]{1,0:T(8,128)S(1)}, u32[]{:S(2)}, u32[]{:S(2)}) collective-permute-start(f32[256,128]{1,0:T(8,128)S(1)} %pad_maximum_fusion.chip_ref.refs_3_), channel_id=1, source_target_pairs={{0,5},{1,14},{2,7},{3,12},{4,1},{5,10},{6,3},{7,8},{8,13},{9,6},{1... | collective-permute-start | bytes 393224 | tf_op jit(solution)/shard_map/ppermute | solution.py:24
  7.8 0.0 collective-permute-done.2.other_ref
  7.8 0.0 copy-start
  7.8 1.2 %copy-done = s32[128,2048]{1,0:T(8,128)S(1)} copy-done((s32[128,2048]{1,0:T(8,128)S(1)}, s32[128,2048]{1,0:T(8,128)}, u32[]{:S(2)}) %copy-start) | copy-done | bytes 1048600
  9.0 0.2 row_operands.1
  9.3 0.0 collective-permute-done.3.refs_4_.refs_3_
  9.3 2.1 %collective-permute-start.6 = (f32[256,128]{1,0:T(8,128)S(1)}, f32[256,128]{1,0:T(8,128)S(1)}, u32[]{:S(2)}, u32[]{:S(2)}) collective-permute-start(f32[256,128]{1,0:T(8,128)S(1)} %collective-permute-done.3.refs_4_.refs_3_), channel_id=1, source_target_pairs={{0,1},{1,4},{2,3},{3,6},{4,5},{5,0},{6,7},{7,2},{8,9},{9,12},{10,1... | collective-permute-start | bytes 393224 | tf_op jit(solution)/shard_map/ppermute | solution.py:24
  11.4 0.0 collective-permute-start.4
  11.4 0.6 %chips_0.1.refs_6_ = f32[64,512]{1,0:T(8,128)S(1)} custom-call(bf16[256,384]{1,0:T(8,128)(2,1)S(1)} %get-tuple-element.19.refs_0_, bf16[256,512]{1,0:T(8,128)(2,1)S(1)} %get-tuple-element.20.refs_1_, f32[4,256,256]{2,1,0:T(8,128)S(1)} %get-tuple-element.21.refs_2_, f32[256,128]{1,0:T(8,128)S(1)} %pad_maximum_fusion.chip_ref.refs_3_, ...), custom_call_target="tpu_custom_call" | custom-call | tf_op jit(solution)/shard_map/chips_0/pallas_call | solution.py:185
  12.0 2.1 %collective-permute-done.5.refs_4_ = f32[256,128]{1,0:T(8,128)S(1)} collective-permute-done((f32[256,128]{1,0:T(8,128)S(1)}, f32[256,128]{1,0:T(8,128)S(1)}, u32[]{:S(2)}, u32[]{:S(2)}) %collective-permute-start.5) | collective-permute-done | bytes 131104 | tf_op jit(solution)/shard_map/ppermute | solution.py:24
  14.1 0.1 collective-permute-done.6.refs_5_
  14.2 1.0 %chips_1.1.refs_4_ = f32[64,512]{1,0:T(8,128)S(1)} custom-call(bf16[256,384]{1,0:T(8,128)(2,1)S(1)} %get-tuple-element.19.refs_0_, bf16[256,512]{1,0:T(8,128)(2,1)S(1)} %get-tuple-element.20.refs_1_, f32[4,256,256]{2,1,0:T(8,128)S(1)} %get-tuple-element.21.refs_2_, f32[256,128]{1,0:T(8,128)S(1)} %collective-permute-done.3.refs_4_.refs_3_, ...), custom_call_target="tpu_custom_call" | custom-call | tf_op jit(solution)/shard_map/chips_1/pallas_call | solution.py:185
  15.2 0.6 %collective-permute-done.4.refs_3_ = f32[256,128]{1,0:T(8,128)S(1)} collective-permute-done((f32[256,128]{1,0:T(8,128)S(1)}, f32[256,128]{1,0:T(8,128)S(1)}, u32[]{:S(2)}, u32[]{:S(2)}) %collective-permute-start.4) | collective-permute-done | bytes 131104 | tf_op jit(solution)/shard_map/ppermute | solution.py:24
  15.8 0.4 %last_chip_1.1 = f32[64,256]{1,0:T(8,128)S(1)} custom-call(bf16[256,384]{1,0:T(8,128)(2,1)S(1)} %get-tuple-element.19.refs_0_, bf16[256,512]{1,0:T(8,128)(2,1)S(1)} %get-tuple-element.20.refs_1_, f32[4,256,256]{2,1,0:T(8,128)S(1)} %get-tuple-element.21.refs_2_, f32[256,128]{1,0:T(8,128)S(1)} %collective-permute-done.4.refs_3_, f32[64,512]{1,0:T(8,128)S(1)} %chips_1.1.refs_4_), custom_call_target="tpu_custom_call" | custom-call | tf_op jit(solution)/shard_map/last_chip_1/pallas_call | solution.py:185
  16.2 0.2 collective-permute-start.7
  16.4 0.4 %last_chip_0.1.mine_ref = f32[64,256]{1,0:T(8,128)S(1)} custom-call(bf16[256,384]{1,0:T(8,128)(2,1)S(1)} %get-tuple-element.19.refs_0_, bf16[256,512]{1,0:T(8,128)(2,1)S(1)} %get-tuple-element.20.refs_1_, f32[4,256,256]{2,1,0:T(8,128)S(1)} %get-tuple-element.21.refs_2_, f32[256,128]{1,0:T(8,128)S(1)} %collective-permute-done.4.refs_3_, ...), custom_call_target="tpu_custom_call" | custom-call | tf_op jit(solution)/shard_map/last_chip_0/pallas_call | solution.py:185
  16.9 0.7 %collective-permute-done.7.got_ref = f32[64,256]{1,0:T(8,128)S(1)} collective-permute-done((f32[64,256]{1,0:T(8,128)S(1)}, f32[64,256]{1,0:T(8,128)S(1)}, u32[]{:S(2)}, u32[]{:S(2)}) %collective-permute-start.7) | collective-permute-done | bytes 65568 | tf_op jit(solution)/shard_map/ppermute | solution.py:24
  17.6 0.1 finish.1
  17.7 8.3 %all_to_all.5.parts_ref = f32[16,1,128]{2,1,0:T(1,128)S(1)} all-to-all(f32[16,1,128]{2,1,0:T(1,128)S(1)} %broadcast_in_dim.9), channel_id=1, replica_groups={{15,14,13,12,11,10,9,8,7,6,5,4,3,2,1,0},{31,30,29,28,27,26,25,24,23,22,..., dimensions={0} | all-to-all | bytes 16384 | tf_op jit(solution)/shard_map/all_to_all | solution.py:282
  26.0 0.7 %results.1 = (f32[64,128]{1,0:T(8,128)}, f32[64,128]{1,0:T(8,128)}, f32[2]{0:T(128)}) custom-call(f32[64,256]{1,0:T(8,128)S(1)} %get-tuple-element.23.total_ref, f32[16,1,128]{2,1,0:T(1,128)S(1)} %all_to_all.5.parts_ref), custom_call_target="tpu_custom_call" | custom-call | tf_op jit(solution)/shard_map/results/pallas_call | solution.py:292
  (2 shorter events, 0.0 us)
Async XLA Ops:
  0.6 1.6 %collective-permute-start = (f32[64,128]{1,0:T(8,128)}, f32[64,128]{1,0:T(8,128)S(1)}, u32[]{:S(2)}, u32[]{:S(2)}) collective-permute-start(f32[64,128]{1,0:T(8,128)} %param.3), channel_id=1, source_target_pairs={{0,1},{1,0},{2,3},{3,2},{4,5},{5,4},{6,7},{7,6},{8,9},{9,8},{10,11... | collective-permute-start | bytes 98312 | tf_op jit(solution)/shard_map/ppermute | solution.py:24
  1.1 1.4 %collective-permute-start.1 = (f32[64,128]{1,0:T(8,128)}, f32[64,128]{1,0:T(8,128)S(1)}, u32[]{:S(2)}, u32[]{:S(2)}) collective-permute-start(f32[64,128]{1,0:T(8,128)} %param.4), channel_id=1, source_target_pairs={{0,1},{1,0},{2,3},{3,2},{4,5},{5,4},{6,7},{7,6},{8,9},{9,8},{10,11... | collective-permute-start | bytes 98312 | tf_op jit(solution)/shard_map/ppermute | solution.py:24
  2.6 5.2 %collective-permute-start.2 = (s32[128,2048]{1,0:T(8,128)}, s32[128,2048]{1,0:T(8,128)S(1)}, u32[]{:S(2)}, u32[]{:S(2)}) collective-permute-start(s32[128,2048]{1,0:T(8,128)} %counts_ref), channel_id=1, source_target_pairs={{0,1},{1,0},{2,3},{3,2},{4,5},{5,4},{6,7},{7,6},{8,9},{9,8},{10,11... | collective-permute-start | bytes 3145736 | tf_op jit(solution)/shard_map/ppermute | solution.py:24
  2.8 6.5 %collective-permute-start.3 = (f32[256,128]{1,0:T(8,128)S(1)}, f32[256,128]{1,0:T(8,128)S(1)}, u32[]{:S(2)}, u32[]{:S(2)}) collective-permute-start(f32[256,128]{1,0:T(8,128)S(1)} %pad_maximum_fusion.chip_ref.refs_3_), channel_id=1, source_target_pairs={{0,2},{1,9},{2,0},{3,11},{4,6},{5,13},{6,4},{7,15},{8,10},{9,1},{1... | collective-permute-start | bytes 393224 | tf_op jit(solution)/shard_map/ppermute | solution.py:24
  5.6 8.5 %collective-permute-start.5 = (f32[256,128]{1,0:T(8,128)S(1)}, f32[256,128]{1,0:T(8,128)S(1)}, u32[]{:S(2)}, u32[]{:S(2)}) collective-permute-start(f32[256,128]{1,0:T(8,128)S(1)} %pad_maximum_fusion.chip_ref.refs_3_), channel_id=1, source_target_pairs={{0,5},{1,14},{2,7},{3,12},{4,1},{5,10},{6,3},{7,8},{8,13},{9,6},{1... | collective-permute-start | bytes 393224 | tf_op jit(solution)/shard_map/ppermute | solution.py:24
  7.8 1.2 %copy-start = (s32[128,2048]{1,0:T(8,128)S(1)}, s32[128,2048]{1,0:T(8,128)}, u32[]{:S(2)}) copy-start(s32[128,2048]{1,0:T(8,128)} %counts_ref) | copy-start | bytes 3145732
  9.3 4.9 %collective-permute-start.6 = (f32[256,128]{1,0:T(8,128)S(1)}, f32[256,128]{1,0:T(8,128)S(1)}, u32[]{:S(2)}, u32[]{:S(2)}) collective-permute-start(f32[256,128]{1,0:T(8,128)S(1)} %collective-permute-done.3.refs_4_.refs_3_), channel_id=1, source_target_pairs={{0,1},{1,4},{2,3},{3,6},{4,5},{5,0},{6,7},{7,2},{8,9},{9,12},{10,1... | collective-permute-start | bytes 393224 | tf_op jit(solution)/shard_map/ppermute | solution.py:24
  11.4 4.4 %collective-permute-start.4 = (f32[256,128]{1,0:T(8,128)S(1)}, f32[256,128]{1,0:T(8,128)S(1)}, u32[]{:S(2)}, u32[]{:S(2)}) collective-permute-start(f32[256,128]{1,0:T(8,128)S(1)} %collective-permute-done.3.refs_4_.refs_3_), channel_id=1, source_target_pairs={{0,5},{1,2},{2,7},{3,0},{4,1},{5,6},{6,3},{7,4},{8,13},{9,10},{10,... | collective-permute-start | bytes 393224 | tf_op jit(solution)/shard_map/ppermute | solution.py:24
  16.2 1.3 %collective-permute-start.7 = (f32[64,256]{1,0:T(8,128)S(1)}, f32[64,256]{1,0:T(8,128)S(1)}, u32[]{:S(2)}, u32[]{:S(2)}) collective-permute-start(f32[64,256]{1,0:T(8,128)S(1)} %last_chip_1.1), channel_id=1, source_target_pairs={{0,1},{1,0},{2,3},{3,2},{4,5},{5,4},{6,7},{7,6},{8,9},{9,8},{10,11... | collective-permute-start | bytes 196616 | tf_op jit(solution)/shard_map/ppermute | solution.py:24

commit v6 on v4

--- a/solution.py
+++ b/solution.py
@@ -284,7 +284,7 @@
         AXES,
         0,
         0,
-        axis_index_groups=[list(range(size))[::-1]],
+        axis_index_groups=[[size - 1, *range(size - 1)]],
         tiled=True,
     )
     return pl.pallas_call(

time: 27 us -> 26.9 us (level)
  no operation moved by 1% of the time
where the time goes in v6:
time: 26.9 us; the launch traced here: 26.7 us
  blocking collectives  8.28 us (31%)
  starting transfers between devices  8.1 us (30%)
  waiting for transfers between devices  3.89 us (14%)
  Pallas kernels  3.67 us (14%)
  local copies, waits for them, and re-layouts  1.23 us (5%)
  other arithmetic  0.79 us (3%)
  between operations  0.72 us (3%)
    all_to_all x1, blocking collectives, local(): lax.all_to_all(jnp.broadcast_to(inner[None], (size, 1, 128)), AXES, 0, 0,...  8.28 us
    ppermute x8, starting transfers between devices, permute(): return lax.ppermute(x, AXES, pairs)  8.1 us
    ppermute x8, waiting for transfers between devices, permute(): return lax.ppermute(x, AXES, pairs)  3.89 us
    pallas_call x7, Pallas kernels, call(): pl.pallas_call(kernel, out_shape=out_shape, in_specs=[vmem] * len(args),...  2.99 us
    unnamed x2, local copies, waits for them, and re-layouts  1.23 us
    concatenate x1, other arithmetic, local(): own = lax.optimization_barrier(jnp.concatenate([factors, tangent], 0))  0.78 us
    pallas_call x1, Pallas kernels, local(): pl.pallas_call(out_kernel, out_shape=(shape(rank, rows), shape(rank, rows...  0.68 us
  transfers between devices with their start and end apart: 8, of which 5 were waited for; matrix products, arithmetic and copies ran while one was open for 3% of the time, Pallas kernels for 9%

profile of v6, /device:TPU:0, one launch (start us, length us, event | category | flops | bytes accessed | tf_op | source)
XLA Modules:
  0.0 26.7 jit_solution(3971219240616350710)
XLA Ops:
  0.6 0.5 %collective-permute-start = (f32[64,128]{1,0:T(8,128)}, f32[64,128]{1,0:T(8,128)S(1)}, u32[]{:S(2)}, u32[]{:S(2)}) collective-permute-start(f32[64,128]{1,0:T(8,128)} %param.3), channel_id=1, source_target_pairs={{0,1},{1,0},{2,3},{3,2},{4,5},{5,4},{6,7},{7,6},{8,9},{9,8},{10,11... | collective-permute-start | bytes 98312 | tf_op jit(solution)/shard_map/ppermute | solution.py:24
  1.1 0.1 collective-permute-start.1
  1.2 0.8 %pad_maximum_fusion.1.own_ref = f32[128,128]{1,0:T(8,128)S(1)} fusion(f32[64,128]{1,0:T(8,128)} %param.4, f32[64,128]{1,0:T(8,128)} %param.3), kind=kLoop, calls=%fused_computation.1 | loop fusion | flops 16384 | bytes 131072 | tf_op jit(solution)/shard_map/concatenate | solution.py:198
  2.0 0.2 collective-permute-done
  2.2 0.3 %collective-permute-done.1 = f32[64,128]{1,0:T(8,128)S(1)} collective-permute-done((f32[64,128]{1,0:T(8,128)}, f32[64,128]{1,0:T(8,128)S(1)}, u32[]{:S(2)}, u32[]{:S(2)}) %collective-permute-start.1) | collective-permute-done | bytes 32800 | tf_op jit(solution)/shard_map/ppermute | solution.py:24
  2.6 0.2 collective-permute-start.2
  2.8 2.8 %collective-permute-start.3 = (f32[256,128]{1,0:T(8,128)S(1)}, f32[256,128]{1,0:T(8,128)S(1)}, u32[]{:S(2)}, u32[]{:S(2)}) collective-permute-start(f32[256,128]{1,0:T(8,128)S(1)} %pad_maximum_fusion.chip_ref.refs_3_), channel_id=1, source_target_pairs={{0,2},{1,9},{2,0},{3,11},{4,6},{5,13},{6,4},{7,15},{8,10},{9,1},{1... | collective-permute-start | bytes 393224 | tf_op jit(solution)/shard_map/ppermute | solution.py:24
  5.6 2.2 %collective-permute-start.5 = (f32[256,128]{1,0:T(8,128)S(1)}, f32[256,128]{1,0:T(8,128)S(1)}, u32[]{:S(2)}, u32[]{:S(2)}) collective-permute-start(f32[256,128]{1,0:T(8,128)S(1)} %pad_maximum_fusion.chip_ref.refs_3_), channel_id=1, source_target_pairs={{0,5},{1,14},{2,7},{3,12},{4,1},{5,10},{6,3},{7,8},{8,13},{9,6},{1... | collective-permute-start | bytes 393224 | tf_op jit(solution)/shard_map/ppermute | solution.py:24
  7.8 0.0 collective-permute-done.2.other_ref
  7.8 0.0 copy-start
  7.8 1.2 %copy-done = s32[128,2048]{1,0:T(8,128)S(1)} copy-done((s32[128,2048]{1,0:T(8,128)S(1)}, s32[128,2048]{1,0:T(8,128)}, u32[]{:S(2)}) %copy-start) | copy-done | bytes 1048600
  9.0 0.2 row_operands.1
  9.3 0.0 collective-permute-done.3.refs_4_.refs_3_
  9.3 2.1 %collective-permute-start.6 = (f32[256,128]{1,0:T(8,128)S(1)}, f32[256,128]{1,0:T(8,128)S(1)}, u32[]{:S(2)}, u32[]{:S(2)}) collective-permute-start(f32[256,128]{1,0:T(8,128)S(1)} %collective-permute-done.3.refs_4_.refs_3_), channel_id=1, source_target_pairs={{0,1},{1,4},{2,3},{3,6},{4,5},{5,0},{6,7},{7,2},{8,9},{9,12},{10,1... | collective-permute-start | bytes 393224 | tf_op jit(solution)/shard_map/ppermute | solution.py:24
  11.4 0.0 collective-permute-start.4
  11.4 0.6 %chips_0.1.refs_5_ = f32[64,512]{1,0:T(8,128)S(1)} custom-call(bf16[256,384]{1,0:T(8,128)(2,1)S(1)} %get-tuple-element.19.refs_0_, bf16[256,512]{1,0:T(8,128)(2,1)S(1)} %get-tuple-element.20.refs_1_, f32[4,256,256]{2,1,0:T(8,128)S(1)} %get-tuple-element.21.refs_2_, f32[256,128]{1,0:T(8,128)S(1)} %pad_maximum_fusion.chip_ref.refs_3_, ...), custom_call_target="tpu_custom_call" | custom-call | tf_op jit(solution)/shard_map/chips_0/pallas_call | solution.py:185
  12.0 2.1 %collective-permute-done.5.refs_4_.refs_3_ = f32[256,128]{1,0:T(8,128)S(1)} collective-permute-done((f32[256,128]{1,0:T(8,128)S(1)}, f32[256,128]{1,0:T(8,128)S(1)}, u32[]{:S(2)}, u32[]{:S(2)}) %collective-permute-start.5) | collective-permute-done | bytes 131104 | tf_op jit(solution)/shard_map/ppermute | solution.py:24
  14.1 0.6 %chips_1.1.refs_5_ = f32[64,512]{1,0:T(8,128)S(1)} custom-call(bf16[256,384]{1,0:T(8,128)(2,1)S(1)} %get-tuple-element.19.refs_0_, bf16[256,512]{1,0:T(8,128)(2,1)S(1)} %get-tuple-element.20.refs_1_, f32[4,256,256]{2,1,0:T(8,128)S(1)} %get-tuple-element.21.refs_2_, f32[256,128]{1,0:T(8,128)S(1)} %collective-permute-done.3.refs_4_.refs_3_, ...), custom_call_target="tpu_custom_call" | custom-call | tf_op jit(solution)/shard_map/chips_1/pallas_call | solution.py:185
  14.7 0.0 collective-permute-done.6.refs_4_
  14.7 0.6 %chips_2.1.refs_4_ = f32[64,512]{1,0:T(8,128)S(1)} custom-call(bf16[256,384]{1,0:T(8,128)(2,1)S(1)} %get-tuple-element.19.refs_0_, bf16[256,512]{1,0:T(8,128)(2,1)S(1)} %get-tuple-element.20.refs_1_, f32[4,256,256]{2,1,0:T(8,128)S(1)} %get-tuple-element.21.refs_2_, f32[256,128]{1,0:T(8,128)S(1)} %collective-permute-done.5.refs_4_.refs_3_, ...), custom_call_target="tpu_custom_call" | custom-call | tf_op jit(solution)/shard_map/chips_2/pallas_call | solution.py:185
  15.3 0.5 %collective-permute-done.4.refs_3_ = f32[256,128]{1,0:T(8,128)S(1)} collective-permute-done((f32[256,128]{1,0:T(8,128)S(1)}, f32[256,128]{1,0:T(8,128)S(1)}, u32[]{:S(2)}, u32[]{:S(2)}) %collective-permute-start.4) | collective-permute-done | bytes 131104 | tf_op jit(solution)/shard_map/ppermute | solution.py:24
  15.8 0.4 %last_chip_1.1 = f32[64,256]{1,0:T(8,128)S(1)} custom-call(bf16[256,384]{1,0:T(8,128)(2,1)S(1)} %get-tuple-element.19.refs_0_, bf16[256,512]{1,0:T(8,128)(2,1)S(1)} %get-tuple-element.20.refs_1_, f32[4,256,256]{2,1,0:T(8,128)S(1)} %get-tuple-element.21.refs_2_, f32[256,128]{1,0:T(8,128)S(1)} %collective-permute-done.4.refs_3_, f32[64,512]{1,0:T(8,128)S(1)} %chips_2.1.refs_4_), custom_call_target="tpu_custom_call" | custom-call | tf_op jit(solution)/shard_map/last_chip_1/pallas_call | solution.py:185
  16.2 0.2 collective-permute-start.7
  16.4 0.4 %last_chip_0.1.mine_ref = f32[64,256]{1,0:T(8,128)S(1)} custom-call(bf16[256,384]{1,0:T(8,128)(2,1)S(1)} %get-tuple-element.19.refs_0_, bf16[256,512]{1,0:T(8,128)(2,1)S(1)} %get-tuple-element.20.refs_1_, f32[4,256,256]{2,1,0:T(8,128)S(1)} %get-tuple-element.21.refs_2_, f32[256,128]{1,0:T(8,128)S(1)} %collective-permute-done.4.refs_3_, ...), custom_call_target="tpu_custom_call" | custom-call | tf_op jit(solution)/shard_map/last_chip_0/pallas_call | solution.py:185
  16.9 0.7 %collective-permute-done.7.got_ref = f32[64,256]{1,0:T(8,128)S(1)} collective-permute-done((f32[64,256]{1,0:T(8,128)S(1)}, f32[64,256]{1,0:T(8,128)S(1)}, u32[]{:S(2)}, u32[]{:S(2)}) %collective-permute-start.7) | collective-permute-done | bytes 65568 | tf_op jit(solution)/shard_map/ppermute | solution.py:24
  17.6 0.1 finish.1
  17.7 8.3 %all_to_all.5.parts_ref = f32[16,1,128]{2,1,0:T(1,128)S(1)} all-to-all(f32[16,1,128]{2,1,0:T(1,128)S(1)} %broadcast_in_dim.9), channel_id=1, replica_groups={{15,0,1,2,3,4,5,6,7,8,9,10,11,12,13,14},{31,16,17,18,19,20,21,22,23,24,..., dimensions={0} | all-to-all | bytes 16384 | tf_op jit(solution)/shard_map/all_to_all | solution.py:282
  26.0 0.7 %results.1 = (f32[64,128]{1,0:T(8,128)}, f32[64,128]{1,0:T(8,128)}, f32[2]{0:T(128)}) custom-call(f32[64,256]{1,0:T(8,128)S(1)} %get-tuple-element.23.total_ref, f32[16,1,128]{2,1,0:T(1,128)S(1)} %all_to_all.5.parts_ref), custom_call_target="tpu_custom_call" | custom-call | tf_op jit(solution)/shard_map/results/pallas_call | solution.py:290
  (2 shorter events, 0.0 us)
Async XLA Ops:
  0.6 1.6 %collective-permute-start = (f32[64,128]{1,0:T(8,128)}, f32[64,128]{1,0:T(8,128)S(1)}, u32[]{:S(2)}, u32[]{:S(2)}) collective-permute-start(f32[64,128]{1,0:T(8,128)} %param.3), channel_id=1, source_target_pairs={{0,1},{1,0},{2,3},{3,2},{4,5},{5,4},{6,7},{7,6},{8,9},{9,8},{10,11... | collective-permute-start | bytes 98312 | tf_op jit(solution)/shard_map/ppermute | solution.py:24
  1.1 1.4 %collective-permute-start.1 = (f32[64,128]{1,0:T(8,128)}, f32[64,128]{1,0:T(8,128)S(1)}, u32[]{:S(2)}, u32[]{:S(2)}) collective-permute-start(f32[64,128]{1,0:T(8,128)} %param.4), channel_id=1, source_target_pairs={{0,1},{1,0},{2,3},{3,2},{4,5},{5,4},{6,7},{7,6},{8,9},{9,8},{10,11... | collective-permute-start | bytes 98312 | tf_op jit(solution)/shard_map/ppermute | solution.py:24
  2.6 5.2 %collective-permute-start.2 = (s32[128,2048]{1,0:T(8,128)}, s32[128,2048]{1,0:T(8,128)S(1)}, u32[]{:S(2)}, u32[]{:S(2)}) collective-permute-start(s32[128,2048]{1,0:T(8,128)} %counts_ref), channel_id=1, source_target_pairs={{0,1},{1,0},{2,3},{3,2},{4,5},{5,4},{6,7},{7,6},{8,9},{9,8},{10,11... | collective-permute-start | bytes 3145736 | tf_op jit(solution)/shard_map/ppermute | solution.py:24
  2.8 6.5 %collective-permute-start.3 = (f32[256,128]{1,0:T(8,128)S(1)}, f32[256,128]{1,0:T(8,128)S(1)}, u32[]{:S(2)}, u32[]{:S(2)}) collective-permute-start(f32[256,128]{1,0:T(8,128)S(1)} %pad_maximum_fusion.chip_ref.refs_3_), channel_id=1, source_target_pairs={{0,2},{1,9},{2,0},{3,11},{4,6},{5,13},{6,4},{7,15},{8,10},{9,1},{1... | collective-permute-start | bytes 393224 | tf_op jit(solution)/shard_map/ppermute | solution.py:24
  5.6 8.5 %collective-permute-start.5 = (f32[256,128]{1,0:T(8,128)S(1)}, f32[256,128]{1,0:T(8,128)S(1)}, u32[]{:S(2)}, u32[]{:S(2)}) collective-permute-start(f32[256,128]{1,0:T(8,128)S(1)} %pad_maximum_fusion.chip_ref.refs_3_), channel_id=1, source_target_pairs={{0,5},{1,14},{2,7},{3,12},{4,1},{5,10},{6,3},{7,8},{8,13},{9,6},{1... | collective-permute-start | bytes 393224 | tf_op jit(solution)/shard_map/ppermute | solution.py:24
  7.8 1.2 %copy-start = (s32[128,2048]{1,0:T(8,128)S(1)}, s32[128,2048]{1,0:T(8,128)}, u32[]{:S(2)}) copy-start(s32[128,2048]{1,0:T(8,128)} %counts_ref) | copy-start | bytes 3145732
  9.3 5.4 %collective-permute-start.6 = (f32[256,128]{1,0:T(8,128)S(1)}, f32[256,128]{1,0:T(8,128)S(1)}, u32[]{:S(2)}, u32[]{:S(2)}) collective-permute-start(f32[256,128]{1,0:T(8,128)S(1)} %collective-permute-done.3.refs_4_.refs_3_), channel_id=1, source_target_pairs={{0,1},{1,4},{2,3},{3,6},{4,5},{5,0},{6,7},{7,2},{8,9},{9,12},{10,1... | collective-permute-start | bytes 393224 | tf_op jit(solution)/shard_map/ppermute | solution.py:24
  11.4 4.4 %collective-permute-start.4 = (f32[256,128]{1,0:T(8,128)S(1)}, f32[256,128]{1,0:T(8,128)S(1)}, u32[]{:S(2)}, u32[]{:S(2)}) collective-permute-start(f32[256,128]{1,0:T(8,128)S(1)} %collective-permute-done.3.refs_4_.refs_3_), channel_id=1, source_target_pairs={{0,5},{1,2},{2,7},{3,0},{4,1},{5,6},{6,3},{7,4},{8,13},{9,10},{10,... | collective-permute-start | bytes 393224 | tf_op jit(solution)/shard_map/ppermute | solution.py:24
  16.2 1.3 %collective-permute-start.7 = (f32[64,256]{1,0:T(8,128)S(1)}, f32[64,256]{1,0:T(8,128)S(1)}, u32[]{:S(2)}, u32[]{:S(2)}) collective-permute-start(f32[64,256]{1,0:T(8,128)S(1)} %last_chip_1.1), channel_id=1, source_target_pairs={{0,1},{1,0},{2,3},{3,2},{4,5},{5,4},{6,7},{7,6},{8,9},{9,8},{10,11... | collective-permute-start | bytes 196616 | tf_op jit(solution)/shard_map/ppermute | solution.py:24

commit v7 on v6

--- a/solution.py
+++ b/solution.py
@@ -176,7 +176,7 @@
     blks, grps = lax.axis_size("blk"), lax.axis_size("grp")
     chips = grps // CORES
     vmem = pl.BlockSpec(memory_space=pltpu.VMEM)
-    params = pltpu.CompilerParams(vmem_limit_bytes=40 * 1024 * 1024)
+    params = pltpu.CompilerParams(vmem_limit_bytes=16 * 1024 * 1024)
 
     def is_far():
         return lax.axis_index("grp") % CORES == FAR

time: 26.9 us -> 26.9 us (level)
  no operation moved by 1% of the time
where the time goes in v7:
time: 26.9 us; the launch traced here: 26.7 us
  blocking collectives  8.28 us (31%)
  starting transfers between devices  8.1 us (30%)
  waiting for transfers between devices  3.89 us (14%)
  Pallas kernels  3.67 us (14%)
  local copies, waits for them, and re-layouts  1.23 us (5%)
  other arithmetic  0.79 us (3%)
  between operations  0.72 us (3%)
    all_to_all x1, blocking collectives, local(): lax.all_to_all(jnp.broadcast_to(inner[None], (size, 1, 128)), AXES, 0, 0,...  8.28 us
    ppermute x8, starting transfers between devices, permute(): return lax.ppermute(x, AXES, pairs)  8.1 us
    ppermute x8, waiting for transfers between devices, permute(): return lax.ppermute(x, AXES, pairs)  3.89 us
    pallas_call x7, Pallas kernels, call(): pl.pallas_call(kernel, out_shape=out_shape, in_specs=[vmem] * len(args),...  2.99 us
    unnamed x2, local copies, waits for them, and re-layouts  1.23 us
    concatenate x1, other arithmetic, local(): own = lax.optimization_barrier(jnp.concatenate([factors, tangent], 0))  0.78 us
    pallas_call x1, Pallas kernels, local(): pl.pallas_call(out_kernel, out_shape=(shape(rank, rows), shape(rank, rows...  0.68 us
  transfers between devices with their start and end apart: 8, of which 5 were waited for; matrix products, arithmetic and copies ran while one was open for 3% of the time, Pallas kernels for 9%

profile of v7, /device:TPU:0, one launch (start us, length us, event | category | flops | bytes accessed | tf_op | source)
XLA Modules:
  0.0 26.7 jit_solution(771157659078409552)
XLA Ops:
  0.6 0.5 %collective-permute-start = (f32[64,128]{1,0:T(8,128)}, f32[64,128]{1,0:T(8,128)S(1)}, u32[]{:S(2)}, u32[]{:S(2)}) collective-permute-start(f32[64,128]{1,0:T(8,128)} %param.3), channel_id=1, source_target_pairs={{0,1},{1,0},{2,3},{3,2},{4,5},{5,4},{6,7},{7,6},{8,9},{9,8},{10,11... | collective-permute-start | bytes 98312 | tf_op jit(solution)/shard_map/ppermute | solution.py:24
  1.1 0.1 collective-permute-start.1
  1.2 0.8 %pad_maximum_fusion.1.own_ref = f32[128,128]{1,0:T(8,128)S(1)} fusion(f32[64,128]{1,0:T(8,128)} %param.4, f32[64,128]{1,0:T(8,128)} %param.3), kind=kLoop, calls=%fused_computation.1 | loop fusion | flops 16384 | bytes 131072 | tf_op jit(solution)/shard_map/concatenate | solution.py:198
  2.0 0.2 collective-permute-done
  2.2 0.3 %collective-permute-done.1 = f32[64,128]{1,0:T(8,128)S(1)} collective-permute-done((f32[64,128]{1,0:T(8,128)}, f32[64,128]{1,0:T(8,128)S(1)}, u32[]{:S(2)}, u32[]{:S(2)}) %collective-permute-start.1) | collective-permute-done | bytes 32800 | tf_op jit(solution)/shard_map/ppermute | solution.py:24
  2.6 0.2 collective-permute-start.2
  2.8 2.8 %collective-permute-start.3 = (f32[256,128]{1,0:T(8,128)S(1)}, f32[256,128]{1,0:T(8,128)S(1)}, u32[]{:S(2)}, u32[]{:S(2)}) collective-permute-start(f32[256,128]{1,0:T(8,128)S(1)} %pad_maximum_fusion.chip_ref.refs_3_), channel_id=1, source_target_pairs={{0,2},{1,9},{2,0},{3,11},{4,6},{5,13},{6,4},{7,15},{8,10},{9,1},{1... | collective-permute-start | bytes 393224 | tf_op jit(solution)/shard_map/ppermute | solution.py:24
  5.6 2.2 %collective-permute-start.5 = (f32[256,128]{1,0:T(8,128)S(1)}, f32[256,128]{1,0:T(8,128)S(1)}, u32[]{:S(2)}, u32[]{:S(2)}) collective-permute-start(f32[256,128]{1,0:T(8,128)S(1)} %pad_maximum_fusion.chip_ref.refs_3_), channel_id=1, source_target_pairs={{0,5},{1,14},{2,7},{3,12},{4,1},{5,10},{6,3},{7,8},{8,13},{9,6},{1... | collective-permute-start | bytes 393224 | tf_op jit(solution)/shard_map/ppermute | solution.py:24
  7.8 0.0 collective-permute-done.2.other_ref
  7.8 0.0 copy-start
  7.8 1.2 %copy-done = s32[128,2048]{1,0:T(8,128)S(1)} copy-done((s32[128,2048]{1,0:T(8,128)S(1)}, s32[128,2048]{1,0:T(8,128)}, u32[]{:S(2)}) %copy-start) | copy-done | bytes 1048600
  9.0 0.2 row_operands.1
  9.3 0.0 collective-permute-done.3.refs_4_.refs_3_
  9.3 2.1 %collective-permute-start.6 = (f32[256,128]{1,0:T(8,128)S(1)}, f32[256,128]{1,0:T(8,128)S(1)}, u32[]{:S(2)}, u32[]{:S(2)}) collective-permute-start(f32[256,128]{1,0:T(8,128)S(1)} %collective-permute-done.3.refs_4_.refs_3_), channel_id=1, source_target_pairs={{0,1},{1,4},{2,3},{3,6},{4,5},{5,0},{6,7},{7,2},{8,9},{9,12},{10,1... | collective-permute-start | bytes 393224 | tf_op jit(solution)/shard_map/ppermute | solution.py:24
  11.4 0.0 collective-permute-start.4
  11.4 0.6 %chips_0.1.refs_5_ = f32[64,512]{1,0:T(8,128)S(1)} custom-call(bf16[256,384]{1,0:T(8,128)(2,1)S(1)} %get-tuple-element.19.refs_0_, bf16[256,512]{1,0:T(8,128)(2,1)S(1)} %get-tuple-element.20.refs_1_, f32[4,256,256]{2,1,0:T(8,128)S(1)} %get-tuple-element.21.refs_2_, f32[256,128]{1,0:T(8,128)S(1)} %pad_maximum_fusion.chip_ref.refs_3_, ...), custom_call_target="tpu_custom_call" | custom-call | tf_op jit(solution)/shard_map/chips_0/pallas_call | solution.py:185
  12.0 2.1 %collective-permute-done.5.refs_4_.refs_3_ = f32[256,128]{1,0:T(8,128)S(1)} collective-permute-done((f32[256,128]{1,0:T(8,128)S(1)}, f32[256,128]{1,0:T(8,128)S(1)}, u32[]{:S(2)}, u32[]{:S(2)}) %collective-permute-start.5) | collective-permute-done | bytes 131104 | tf_op jit(solution)/shard_map/ppermute | solution.py:24
  14.1 0.6 %chips_1.1.refs_5_ = f32[64,512]{1,0:T(8,128)S(1)} custom-call(bf16[256,384]{1,0:T(8,128)(2,1)S(1)} %get-tuple-element.19.refs_0_, bf16[256,512]{1,0:T(8,128)(2,1)S(1)} %get-tuple-element.20.refs_1_, f32[4,256,256]{2,1,0:T(8,128)S(1)} %get-tuple-element.21.refs_2_, f32[256,128]{1,0:T(8,128)S(1)} %collective-permute-done.3.refs_4_.refs_3_, ...), custom_call_target="tpu_custom_call" | custom-call | tf_op jit(solution)/shard_map/chips_1/pallas_call | solution.py:185
  14.7 0.0 collective-permute-done.6.refs_4_
  14.7 0.6 %chips_2.1.refs_4_ = f32[64,512]{1,0:T(8,128)S(1)} custom-call(bf16[256,384]{1,0:T(8,128)(2,1)S(1)} %get-tuple-element.19.refs_0_, bf16[256,512]{1,0:T(8,128)(2,1)S(1)} %get-tuple-element.20.refs_1_, f32[4,256,256]{2,1,0:T(8,128)S(1)} %get-tuple-element.21.refs_2_, f32[256,128]{1,0:T(8,128)S(1)} %collective-permute-done.5.refs_4_.refs_3_, ...), custom_call_target="tpu_custom_call" | custom-call | tf_op jit(solution)/shard_map/chips_2/pallas_call | solution.py:185
  15.3 0.5 %collective-permute-done.4.refs_3_ = f32[256,128]{1,0:T(8,128)S(1)} collective-permute-done((f32[256,128]{1,0:T(8,128)S(1)}, f32[256,128]{1,0:T(8,128)S(1)}, u32[]{:S(2)}, u32[]{:S(2)}) %collective-permute-start.4) | collective-permute-done | bytes 131104 | tf_op jit(solution)/shard_map/ppermute | solution.py:24
  15.8 0.4 %last_chip_1.1 = f32[64,256]{1,0:T(8,128)S(1)} custom-call(bf16[256,384]{1,0:T(8,128)(2,1)S(1)} %get-tuple-element.19.refs_0_, bf16[256,512]{1,0:T(8,128)(2,1)S(1)} %get-tuple-element.20.refs_1_, f32[4,256,256]{2,1,0:T(8,128)S(1)} %get-tuple-element.21.refs_2_, f32[256,128]{1,0:T(8,128)S(1)} %collective-permute-done.4.refs_3_, f32[64,512]{1,0:T(8,128)S(1)} %chips_2.1.refs_4_), custom_call_target="tpu_custom_call" | custom-call | tf_op jit(solution)/shard_map/last_chip_1/pallas_call | solution.py:185
  16.2 0.2 collective-permute-start.7
  16.4 0.4 %last_chip_0.1.mine_ref = f32[64,256]{1,0:T(8,128)S(1)} custom-call(bf16[256,384]{1,0:T(8,128)(2,1)S(1)} %get-tuple-element.19.refs_0_, bf16[256,512]{1,0:T(8,128)(2,1)S(1)} %get-tuple-element.20.refs_1_, f32[4,256,256]{2,1,0:T(8,128)S(1)} %get-tuple-element.21.refs_2_, f32[256,128]{1,0:T(8,128)S(1)} %collective-permute-done.4.refs_3_, ...), custom_call_target="tpu_custom_call" | custom-call | tf_op jit(solution)/shard_map/last_chip_0/pallas_call | solution.py:185
  16.9 0.7 %collective-permute-done.7.got_ref = f32[64,256]{1,0:T(8,128)S(1)} collective-permute-done((f32[64,256]{1,0:T(8,128)S(1)}, f32[64,256]{1,0:T(8,128)S(1)}, u32[]{:S(2)}, u32[]{:S(2)}) %collective-permute-start.7) | collective-permute-done | bytes 65568 | tf_op jit(solution)/shard_map/ppermute | solution.py:24
  17.6 0.1 finish.1
  17.7 8.3 %all_to_all.5.parts_ref = f32[16,1,128]{2,1,0:T(1,128)S(1)} all-to-all(f32[16,1,128]{2,1,0:T(1,128)S(1)} %broadcast_in_dim.9), channel_id=1, replica_groups={{15,0,1,2,3,4,5,6,7,8,9,10,11,12,13,14},{31,16,17,18,19,20,21,22,23,24,..., dimensions={0} | all-to-all | bytes 16384 | tf_op jit(solution)/shard_map/all_to_all | solution.py:282
  26.0 0.7 %results.1 = (f32[64,128]{1,0:T(8,128)}, f32[64,128]{1,0:T(8,128)}, f32[2]{0:T(128)}) custom-call(f32[64,256]{1,0:T(8,128)S(1)} %get-tuple-element.23.total_ref, f32[16,1,128]{2,1,0:T(1,128)S(1)} %all_to_all.5.parts_ref), custom_call_target="tpu_custom_call" | custom-call | tf_op jit(solution)/shard_map/results/pallas_call | solution.py:290
  (2 shorter events, 0.0 us)
Async XLA Ops:
  0.6 1.6 %collective-permute-start = (f32[64,128]{1,0:T(8,128)}, f32[64,128]{1,0:T(8,128)S(1)}, u32[]{:S(2)}, u32[]{:S(2)}) collective-permute-start(f32[64,128]{1,0:T(8,128)} %param.3), channel_id=1, source_target_pairs={{0,1},{1,0},{2,3},{3,2},{4,5},{5,4},{6,7},{7,6},{8,9},{9,8},{10,11... | collective-permute-start | bytes 98312 | tf_op jit(solution)/shard_map/ppermute | solution.py:24
  1.1 1.4 %collective-permute-start.1 = (f32[64,128]{1,0:T(8,128)}, f32[64,128]{1,0:T(8,128)S(1)}, u32[]{:S(2)}, u32[]{:S(2)}) collective-permute-start(f32[64,128]{1,0:T(8,128)} %param.4), channel_id=1, source_target_pairs={{0,1},{1,0},{2,3},{3,2},{4,5},{5,4},{6,7},{7,6},{8,9},{9,8},{10,11... | collective-permute-start | bytes 98312 | tf_op jit(solution)/shard_map/ppermute | solution.py:24
  2.6 5.2 %collective-permute-start.2 = (s32[128,2048]{1,0:T(8,128)}, s32[128,2048]{1,0:T(8,128)S(1)}, u32[]{:S(2)}, u32[]{:S(2)}) collective-permute-start(s32[128,2048]{1,0:T(8,128)} %counts_ref), channel_id=1, source_target_pairs={{0,1},{1,0},{2,3},{3,2},{4,5},{5,4},{6,7},{7,6},{8,9},{9,8},{10,11... | collective-permute-start | bytes 3145736 | tf_op jit(solution)/shard_map/ppermute | solution.py:24
  2.8 6.5 %collective-permute-start.3 = (f32[256,128]{1,0:T(8,128)S(1)}, f32[256,128]{1,0:T(8,128)S(1)}, u32[]{:S(2)}, u32[]{:S(2)}) collective-permute-start(f32[256,128]{1,0:T(8,128)S(1)} %pad_maximum_fusion.chip_ref.refs_3_), channel_id=1, source_target_pairs={{0,2},{1,9},{2,0},{3,11},{4,6},{5,13},{6,4},{7,15},{8,10},{9,1},{1... | collective-permute-start | bytes 393224 | tf_op jit(solution)/shard_map/ppermute | solution.py:24
  5.6 8.5 %collective-permute-start.5 = (f32[256,128]{1,0:T(8,128)S(1)}, f32[256,128]{1,0:T(8,128)S(1)}, u32[]{:S(2)}, u32[]{:S(2)}) collective-permute-start(f32[256,128]{1,0:T(8,128)S(1)} %pad_maximum_fusion.chip_ref.refs_3_), channel_id=1, source_target_pairs={{0,5},{1,14},{2,7},{3,12},{4,1},{5,10},{6,3},{7,8},{8,13},{9,6},{1... | collective-permute-start | bytes 393224 | tf_op jit(solution)/shard_map/ppermute | solution.py:24
  7.8 1.2 %copy-start = (s32[128,2048]{1,0:T(8,128)S(1)}, s32[128,2048]{1,0:T(8,128)}, u32[]{:S(2)}) copy-start(s32[128,2048]{1,0:T(8,128)} %counts_ref) | copy-start | bytes 3145732
  9.3 5.4 %collective-permute-start.6 = (f32[256,128]{1,0:T(8,128)S(1)}, f32[256,128]{1,0:T(8,128)S(1)}, u32[]{:S(2)}, u32[]{:S(2)}) collective-permute-start(f32[256,128]{1,0:T(8,128)S(1)} %collective-permute-done.3.refs_4_.refs_3_), channel_id=1, source_target_pairs={{0,1},{1,4},{2,3},{3,6},{4,5},{5,0},{6,7},{7,2},{8,9},{9,12},{10,1... | collective-permute-start | bytes 393224 | tf_op jit(solution)/shard_map/ppermute | solution.py:24
  11.4 4.4 %collective-permute-start.4 = (f32[256,128]{1,0:T(8,128)S(1)}, f32[256,128]{1,0:T(8,128)S(1)}, u32[]{:S(2)}, u32[]{:S(2)}) collective-permute-start(f32[256,128]{1,0:T(8,128)S(1)} %collective-permute-done.3.refs_4_.refs_3_), channel_id=1, source_target_pairs={{0,5},{1,2},{2,7},{3,0},{4,1},{5,6},{6,3},{7,4},{8,13},{9,10},{10,... | collective-permute-start | bytes 393224 | tf_op jit(solution)/shard_map/ppermute | solution.py:24
  16.2 1.3 %collective-permute-start.7 = (f32[64,256]{1,0:T(8,128)S(1)}, f32[64,256]{1,0:T(8,128)S(1)}, u32[]{:S(2)}, u32[]{:S(2)}) collective-permute-start(f32[64,256]{1,0:T(8,128)S(1)} %last_chip_1.1), channel_id=1, source_target_pairs={{0,1},{1,0},{2,3},{3,2},{4,5},{5,4},{6,7},{7,6},{8,9},{9,8},{10,11... | collective-permute-start | bytes 196616 | tf_op jit(solution)/shard_map/ppermute | solution.py:24
